TPU v7x, 32 devices: a whole 2x2x4 slice. The times are simulated.
32 devices in a mesh: dp: 4 (over y, core), expert: 8 (over z, x).
Axes of the slice: x: 2, y: 2, z: 4, core: 2. Of those that a mesh axis runs over, the one named last changes fastest.
Arguments:
- tokens: bfloat16 [32, 576, 768], P(('dp', 'expert')), may hold values from -6 to 6
- segment_ids: int32 [32, 576], P(('dp', 'expert')), may hold values from 0 to 3, never falling along the last dimension, each value on 1 to 288 neighbouring positions
- pad_mask: int32 [32, 576], P(('dp', 'expert')), may hold values 0 or 1
- routes: int32 [32, 576, 2], P(('dp', 'expert')), may hold values from 0 to 7, all different within a row; in each aligned block of 576 rows (0 to 575, 576 to 1151, ..., all dimensions but the last counted through in order) at most 288 rows name the same one
- priority: int32 [32, 576], P(('dp', 'expert')), may hold values from 0 to 63
- gain_attn: float32 [768], replicated, may hold values from 0.5 to 1.5
- w_qkv: bfloat16 [768, 2304], replicated, may hold values from -0.21875 to 0.21875
- w_o: bfloat16 [768, 768], replicated, may hold values from -1.75 to 1.75
- gain_moe: float32 [768], replicated, may hold values from 0.5 to 1.5
- w_router: bfloat16 [768, 8], replicated, may hold values from -0.15625 to 0.15625
- w_in: bfloat16 [8, 768, 3072], P('expert', None, 'dp'), may hold values from -0.21875 to 0.21875
- w_out: bfloat16 [8, 3072, 768], P('expert', 'dp'), may hold values from -0.4375 to 0.4375
- cotangent: bfloat16 [32, 576, 768], P(('dp', 'expert')), may hold values from -6 to 6
Outputs:
- block_out: bfloat16 [32, 576, 768], P(('dp', 'expert'))
- grad_tokens: float32 [32, 576, 768], P(('dp', 'expert'))
- grad_gain_attn: float32 [768], replicated
- grad_w_qkv: float32 [768, 2304], replicated
- grad_w_o: float32 [768, 768], replicated
- grad_gain_moe: float32 [768], replicated
- grad_w_router: float32 [768, 8], replicated
- grad_w_in: float32 [8, 768, 3072], P('expert', None, 'dp')
- grad_w_out: float32 [8, 3072, 768], P('expert', 'dp')
Inputs may be any that keep to these rules, and one draw needn't show every extreme that they name: `routes`: in each aligned block of 576 patches (one device's patches) no expert is named by more than 288 pairs, a bound that some block reaches; the two experts of a patch differ. `segment_ids`: never falling along a row.
All inputs are finite; a program needn't handle non-finite values. No bound on the sum of `pad_mask` on one device may be relied on, other than what follows from the above.
Results may differ from a plain program's by a relative error of at most 0.014.
Values may be sent and summed in bfloat16 or wider, within the bound.
No kernel may reach another device: no remote copies, remote signals or barrier semaphores. Data moves between devices by JAX's collectives and lax.ppermute only.
A program may use at most 256 MiB of HBM per device.

v0:
```python
import jax
import jax.numpy as jnp
from jax import lax
from jax.sharding import PartitionSpec as P

HEADS = 12
HEAD_DIM = 64
LEVELS = 64


def layer_norm(values, gain_vector):
    center = values - jnp.mean(values, axis=-1, keepdims=True)
    spread = jnp.mean(center * center, axis=-1, keepdims=True)
    return center * lax.rsqrt(spread + 1e-06) * gain_vector


def contract(left_side, right_side, left_dim, right_dim):
    return lax.dot_general(
        left_side,
        right_side,
        (((left_dim,), (right_dim,)), ((), ())),
        preferred_element_type=jnp.float32,
    )


def smooth(values):
    return jax.nn.gelu(values, approximate=True)


def split_heads(projected):
    length = projected.shape[0]
    parts = projected.reshape(length, 3, HEADS, HEAD_DIM)
    return (parts[:, 0], parts[:, 1], parts[:, 2])


def masked_scores(queries, key_rows, segment, padding):
    length = segment.shape[0]
    places = jnp.arange(length)
    allowed = (segment[:, None] == segment[None, :]) & (
        (padding[None, :] > 0) | (places[:, None] == places[None, :])
    )
    raw_scores = jnp.einsum("qhd,khd->hqk", queries, key_rows, preferred_element_type=jnp.float32)
    return jnp.where(allowed[None], raw_scores * HEAD_DIM ** (-0.5), -1e30)


def attend_forward(packed, gain_attn, w_qkv, w_o):
    row_values, segment, padding = packed
    length, features = row_values.shape
    residual = row_values.astype(jnp.float32)
    normed = layer_norm(residual, gain_attn).astype(jnp.bfloat16)
    projected = jnp.dot(normed, w_qkv, preferred_element_type=jnp.float32).astype(jnp.bfloat16)
    queries, key_rows, value_rows = split_heads(projected)
    scores = masked_scores(queries, key_rows, segment, padding)
    row_top = jnp.max(scores, axis=-1, keepdims=True)
    exponent = jnp.exp(scores - row_top)
    row_total = jnp.sum(exponent, axis=-1, keepdims=True)
    attention = (exponent / row_total).astype(jnp.bfloat16)
    mixture = jnp.einsum("hqk,khd->qhd", attention, value_rows, preferred_element_type=jnp.float32)
    mixture = mixture.astype(jnp.bfloat16).reshape(length, features)
    hidden = residual + jnp.dot(mixture, w_o, preferred_element_type=jnp.float32)
    return (hidden, normed, projected, mixture, row_top + jnp.log(row_total))


def attend_backward(packed, gain_attn, w_qkv, w_o):
    row_values, segment, padding, normed, projected, mixture, logsum, grad_hidden = packed
    length, features = row_values.shape
    grad_branch = grad_hidden.astype(jnp.bfloat16)
    grad_o = contract(mixture, grad_branch, 0, 0)
    grad_mixture = (
        contract(grad_branch, w_o, 1, 1).astype(jnp.bfloat16).reshape(length, HEADS, HEAD_DIM)
    )
    queries, key_rows, value_rows = split_heads(projected)
    scores = masked_scores(queries, key_rows, segment, padding)
    attention = jnp.exp(scores - logsum)
    grad_attention = jnp.einsum(
        "qhd,khd->hqk", grad_mixture, value_rows, preferred_element_type=jnp.float32
    )
    centered = grad_attention - jnp.sum(attention * grad_attention, axis=-1, keepdims=True)
    grad_scores = (attention * centered * HEAD_DIM ** (-0.5)).astype(jnp.bfloat16)
    grad_value = jnp.einsum(
        "hqk,qhd->khd",
        attention.astype(jnp.bfloat16),
        grad_mixture,
        preferred_element_type=jnp.float32,
    )
    grad_query = jnp.einsum(
        "hqk,khd->qhd", grad_scores, key_rows, preferred_element_type=jnp.float32
    )
    grad_key = jnp.einsum("hqk,qhd->khd", grad_scores, queries, preferred_element_type=jnp.float32)
    grad_projected = (
        jnp.stack([grad_query, grad_key, grad_value], axis=1)
        .reshape(length, 3 * features)
        .astype(jnp.bfloat16)
    )
    grad_qkv = contract(normed, grad_projected, 0, 0)
    grad_normed = contract(grad_projected, w_qkv, 1, 1)
    residual = row_values.astype(jnp.float32)
    unused, pullback = jax.vjp(layer_norm, residual, gain_attn)
    grad_residual, grad_gain = pullback(grad_normed)
    return (grad_hidden + grad_residual, grad_qkv, grad_o, grad_gain)


def expert_forward(in_rows, w_first, w_second):
    preact = jnp.einsum("erd,edf->erf", in_rows, w_first, preferred_element_type=jnp.float32)
    active = smooth(preact).astype(jnp.bfloat16)
    return jnp.einsum("erf,efd->erd", active, w_second, preferred_element_type=jnp.float32)


def expert_backward(in_rows, grad_out_rows, w_first, w_second):
    preact = jnp.einsum("erd,edf->erf", in_rows, w_first, preferred_element_type=jnp.float32)
    active, pullback = jax.vjp(smooth, preact)
    grad_active = jnp.einsum(
        "erd,efd->erf", grad_out_rows, w_second, preferred_element_type=jnp.float32
    )
    grad_preact = pullback(grad_active)[0].astype(jnp.bfloat16)
    grad_first = jnp.einsum(
        "erd,erf->edf", in_rows, grad_preact, preferred_element_type=jnp.float32
    )
    grad_second = jnp.einsum(
        "erf,erd->efd",
        active.astype(jnp.bfloat16),
        grad_out_rows,
        preferred_element_type=jnp.float32,
    )
    grad_in_rows = jnp.einsum(
        "erf,edf->erd", grad_preact, w_first, preferred_element_type=jnp.float32
    )
    return (grad_in_rows, grad_first, grad_second)


def local(
    tokens,
    segment_ids,
    pad_mask,
    routes,
    priority,
    gain_attn,
    w_qkv,
    w_o,
    gain_moe,
    w_router,
    w_in,
    w_out,
    cotangent,
):
    sequences, length, features = tokens.shape
    tok_count = sequences * length
    pair_count = 2 * tok_count
    experts = w_router.shape[1]
    groups = lax.axis_size("expert")
    slot_count = 4 * tok_count // experts
    all_tokens = tok_count * lax.axis_size("dp") * groups
    capacity = (42 * all_tokens + 20 * experts - 1) // (20 * experts)
    bin_count = 2 * LEVELS
    hidden, normed, projected, mixture, logsum = lax.map(
        lambda packed: attend_forward(packed, gain_attn, w_qkv, w_o),
        (tokens, segment_ids, pad_mask),
    )
    flat_hidden = hidden.reshape(tok_count, features)
    normed_moe = layer_norm(flat_hidden, gain_moe).astype(jnp.bfloat16)
    router = jax.nn.softmax(
        jnp.dot(normed_moe, w_router, preferred_element_type=jnp.float32), axis=-1
    )
    pair_expert = routes.reshape(pair_count)
    pair_order = jnp.arange(pair_count)
    pair_token = pair_order // 2
    valid_pair = jnp.repeat(pad_mask.reshape(tok_count), 2) > 0
    pair_class = pair_order % 2 * LEVELS + (LEVELS - 1) - jnp.repeat(priority.reshape(tok_count), 2)
    expert_match = pair_expert[:, None] == jnp.arange(experts)[None, :]
    expert_hot = (expert_match & valid_pair[:, None]).astype(jnp.int32)
    class_hot = (pair_class[:, None] == jnp.arange(bin_count)[None, :]).astype(jnp.int32)
    histogram = jnp.einsum("pe,pb->eb", expert_hot, class_hot)
    my_index = lax.axis_index(("dp", "expert"))
    every_count = lax.all_gather(histogram[None], ("dp", "expert"), axis=0, tiled=True)
    lower = (jnp.arange(every_count.shape[0]) < my_index)[:, None, None]
    before = jnp.sum(jnp.where(lower, every_count, 0), axis=0)
    totals = jnp.sum(every_count, axis=0)
    base_table = jnp.cumsum(totals, axis=1) - totals + before
    base_rank = jnp.sum(jnp.einsum("pe,eb->pb", expert_hot, base_table) * class_hot, axis=1)
    pair_code = pair_expert * bin_count + pair_class
    same_code = (
        (pair_code[:, None] == pair_code[None, :])
        & (pair_token[None, :] < pair_token[:, None])
        & valid_pair[None, :]
    )
    pair_rank = base_rank + jnp.sum(same_code.astype(jnp.int32), axis=1)
    kept_pair = valid_pair & (pair_rank < capacity)
    same_expert = (
        (pair_expert[:, None] == pair_expert[None, :])
        & (pair_order[None, :] < pair_order[:, None])
        & kept_pair[None, :]
    )
    slot_index = jnp.sum(same_expert.astype(jnp.int32), axis=1)
    target = jnp.where(kept_pair, pair_expert * slot_count + slot_index, experts * slot_count)
    safe_target = jnp.minimum(target, experts * slot_count - 1)
    pair_rows = jnp.repeat(normed_moe, 2, axis=0)
    send_buffer = (
        jnp.zeros((experts * slot_count, features), jnp.bfloat16)
        .at[target]
        .set(pair_rows, mode="drop")
    )
    received = lax.all_to_all(
        send_buffer.reshape(experts, slot_count, features),
        "expert",
        split_axis=0,
        concat_axis=1,
        tiled=True,
    )
    full_in, full_out = (
        lax.all_gather(w_in, "dp", axis=2, tiled=True),
        lax.all_gather(w_out, "dp", axis=1, tiled=True),
    )
    result = expert_forward(received, full_in, full_out).astype(jnp.bfloat16)
    returned = lax.all_to_all(result, "expert", split_axis=1, concat_axis=0, tiled=True).reshape(
        experts * slot_count, features
    )
    picked = jnp.where(kept_pair[:, None], returned[safe_target].astype(jnp.float32), 0.0)
    gate_hot = expert_match.astype(jnp.float32)
    gate_value = jnp.sum(gate_hot * jnp.repeat(router, 2, axis=0), axis=1)
    weight = jnp.where(kept_pair, gate_value, 0.0)
    expert_sum = jnp.sum((weight[:, None] * picked).reshape(tok_count, 2, features), axis=1)
    block_out = (flat_hidden + expert_sum).reshape(sequences, length, features).astype(jnp.bfloat16)
    grad_flat = cotangent.reshape(tok_count, features).astype(jnp.float32)
    grad_pairs = jnp.repeat(grad_flat, 2, axis=0)
    grad_gate = jnp.where(kept_pair, jnp.sum(grad_pairs * picked, axis=1), 0.0)
    grad_slots = (weight[:, None] * grad_pairs).astype(jnp.bfloat16)
    grad_buffer = (
        jnp.zeros((experts * slot_count, features), jnp.bfloat16)
        .at[target]
        .set(grad_slots, mode="drop")
    )
    grad_received = lax.all_to_all(
        grad_buffer.reshape(experts, slot_count, features),
        "expert",
        split_axis=0,
        concat_axis=1,
        tiled=True,
    )
    grad_full, grad_full_in, grad_full_out = expert_backward(
        received, grad_received, full_in, full_out
    )
    grad_in, grad_out = (
        lax.psum_scatter(
            grad_full_in.astype(jnp.bfloat16), "dp", scatter_dimension=2, tiled=True
        ).astype(jnp.float32),
        lax.psum_scatter(
            grad_full_out.astype(jnp.bfloat16), "dp", scatter_dimension=1, tiled=True
        ).astype(jnp.float32),
    )
    grad_rows = grad_full.astype(jnp.bfloat16)
    grad_returned = lax.all_to_all(
        grad_rows, "expert", split_axis=1, concat_axis=0, tiled=True
    ).reshape(experts * slot_count, features)
    grad_pair_rows = jnp.where(
        kept_pair[:, None], grad_returned[safe_target].astype(jnp.float32), 0.0
    )
    grad_normed_moe = jnp.sum(grad_pair_rows.reshape(tok_count, 2, features), axis=1)
    grad_router = jnp.sum((gate_hot * grad_gate[:, None]).reshape(tok_count, 2, experts), axis=1)
    grad_logits = (
        router * (grad_router - jnp.sum(router * grad_router, axis=1, keepdims=True))
    ).astype(jnp.bfloat16)
    grad_w_router = contract(normed_moe, grad_logits, 0, 0)
    grad_normed_moe = grad_normed_moe + contract(grad_logits, w_router, 1, 1)
    unused, pullback = jax.vjp(layer_norm, flat_hidden, gain_moe)
    grad_residual, grad_gain_moe = pullback(grad_normed_moe)
    grad_hidden = (grad_flat + grad_residual).reshape(sequences, length, features)
    grad_tokens, grad_qkv, grad_o, grad_gain_attn = lax.map(
        lambda packed: attend_backward(packed, gain_attn, w_qkv, w_o),
        (tokens, segment_ids, pad_mask, normed, projected, mixture, logsum, grad_hidden),
    )
    summed = lax.psum(
        (
            jnp.sum(grad_qkv, axis=0),
            jnp.sum(grad_o, axis=0),
            grad_w_router,
            jnp.sum(grad_gain_attn, axis=0),
            grad_gain_moe,
        ),
        ("dp", "expert"),
    )
    return (
        block_out,
        grad_tokens,
        summed[3],
        summed[0],
        summed[1],
        summed[4],
        summed[2],
        grad_in,
        grad_out,
    )


def solution(mesh):
    return jax.shard_map(
        local,
        mesh=mesh,
        in_specs=(
            P(("dp", "expert"), None, None),
            P(("dp", "expert"), None),
            P(("dp", "expert"), None),
            P(("dp", "expert"), None, None),
            P(("dp", "expert"), None),
            P(),
            P(),
            P(),
            P(),
            P(),
            P("expert", None, "dp"),
            P("expert", "dp", None),
            P(("dp", "expert"), None, None),
        ),
        out_specs=(
            P(("dp", "expert"), None, None),
            P(("dp", "expert"), None, None),
            P(),
            P(),
            P(),
            P(),
            P(),
            P("expert", None, "dp"),
            P("expert", "dp", None),
        ),
        check_vma=False,
    )
```

profile of v0, /device:TPU:0, one launch (start us, length us, event | category | flops | bytes accessed | tf_op | source)
XLA Modules:
  0.0 1224.4 jit_solution(17957616342905147654)
XLA Ops:
  32.6 70.5 %all-gather = s32[256,128]{1,0:T(8,128)S(1)} all-gather(s32[8,128]{1,0:T(8,128)S(1)} %fusion.89), channel_id=2, replica_groups=mesh['dp'=4,'expert'=8] {'dp','expert'}, dimensions={0}, use_global_device_ids=true | all-gather | bytes 135168 | tf_op jit(solution)/shard_map/all_gather | solution.py:174
  117.8 11.2 fusion.123
  129.0 9.1 fusion.9
  138.1 9.7 fusion.75
  165.3 11.0 scatter_custom_fusion
  181.6 74.5 %all-to-all-done = bf16[8,288,768]{2,1,0:T(8,128)(2,1)} async-done(((bf16[8,288,768]{2,1,0:T(8,128)(2,1)}), bf16[8,288,768]{2,1,0:T(8,128)(2,1)}, u32[]{:S(2)}, u32[]{:S(2)}) %all-to-all-start) | async-done | bytes 3538976 | tf_op jit(solution)/shard_map/all_to_all | solution.py:202
  256.1 26.8 %multiply_convert_fusion = (bf16[2304,3072]{1,0:T(8,128)(2,1)}, f32[2304,3072]{1,0:T(8,128)}) fusion(bf16[2304,768]{1,0:T(8,128)(2,1)} %bitcast.10, bf16[1,768,3072]{2,1,0:T(8,128)(2,1)} %all-gather.4.cloned.1.call-done), kind=kOutput, calls=%fused_computation.14 | convolution fusion | flops 10935336960 | bytes 50724864 | tf_op jit(solution)/shard_map/erd,edf->erf/dot_general | solution.py:104
  283.0 15.2 %fusion.36 = bf16[1,2304,768]{2,1,0:T(8,128)(2,1)S(1)} fusion(bf16[2304,3072]{1,0:T(8,128)(2,1)} %get-tuple-element.121, bf16[1,3072,768]{2,1,0:T(8,128)(2,1)} %all-gather.6.cloned.1.call-done), kind=kOutput, calls=%fused_computation.49 | convolution fusion | flops 10873405440 | bytes 22413312 | tf_op jit(solution)/shard_map/erf,efd->erd/dot_general | solution.py:106
  298.2 26.9 %copy.98 = bf16[1,2304,768]{2,0,1:T(2,128)(2,1)} copy(bf16[1,2304,768]{2,1,0:T(8,128)(2,1)S(1)} %fusion.36) | data formatting | bytes 7077888 | tf_op jit(solution)/shard_map/convert_element_type | solution.py:213
  325.7 77.0 %reduce.14 = bf16[2304,768]{1,0:T(8,128)(2,1)} reduce(bf16[2304,1,768]{2,1,0:T(2,128)(2,1)} %bitcast.161, bf16[]{:T(256)} %broadcast.596), dimensions={1}, to_apply=%bitcast.156.reduce_sub_computation | reduce | bytes 7077890
  402.7 6.6 reshape.689
  432.1 60.1 %all-to-all-done.1 = bf16[8,2,110592]{2,1,0:T(2,128)(2,1)} async-done(((bf16[8,2,110592]{2,1,0:T(2,128)(2,1)}), bf16[8,2,110592]{2,1,0:T(2,128)(2,1)}, u32[]{:S(2)}, u32[]{:S(2)}) %all-to-all-start.1) | async-done | bytes 3538976 | tf_op jit(solution)/shard_map/all_to_all | solution.py:214
  492.2 8.1 reshape.690
  505.9 8.2 gather_fusion
  527.3 12.5 %scatter_custom_fusion.1 = bf16[2304,768]{1,0:T(8,128)(2,1)} fusion(s32[1152]{0:T(1024)} %copy-done.46, f32[1152,768]{1,0:T(8,128)} %reshape.639, f32[1152]{0:T(1024)} %broadcast_select_fusion, bf16[]{:T(256)} %constant.164.clone.1), kind=kCustom, calls=%fused_computation.80 | custom fusion | flops 1769472 | bytes 7086592 | tf_op jit(solution)/shard_map/scatter | solution.py:230
  539.8 83.3 %all_to_all.16 = bf16[8,288,768]{2,1,0:T(8,128)(2,1)S(1)} all-to-all(bf16[8,288,768]{2,1,0:T(8,128)(2,1)} %bitcast.165), channel_id=1, replica_groups=mesh['dp'=4,'expert'=8] {'expert'}, dimensions={0} | all-to-all | bytes 7077888 | tf_op jit(solution)/shard_map/all_to_all | solution.py:232
  624.9 15.9 %fusion.42 = bf16[1,3072,768]{2,1,0:T(8,128)(2,1)} fusion(bf16[2304,3072]{1,0:T(8,128)(2,1)} %get-tuple-element.121, bf16[2304,768]{1,0:T(8,128)(2,1)S(1)} %bitcast.174), kind=kOutput, calls=%fused_computation.51 | convolution fusion | flops 10873995264 | bytes 22413312 | tf_op jit(solution)/shard_map/erf,erd->efd/dot_general | solution.py:119
  640.9 35.9 %fusion.7 = bf16[2304,3072]{1,0:T(8,128)(2,1)} fusion(f32[2304,3072]{1,0:T(8,128)} %get-tuple-element.122, bf16[2304,768]{1,0:T(8,128)(2,1)} %bitcast.175, bf16[1,3072,768]{2,1,0:T(8,128)(2,1)} %all-gather.6.cloned.1.call-done), kind=kOutput, calls=%fused_computation.13 | convolution fusion | flops 11013193728 | bytes 50724864 | tf_op jit(solution)/shard_map/erd,efd->erf/dot_general | solution.py:112
  676.8 15.4 %fusion.39 = bf16[1,2304,768]{2,1,0:T(8,128)(2,1)S(1)} fusion(bf16[2304,3072]{1,0:T(8,128)(2,1)} %fusion.7, bf16[1,768,3072]{2,1,0:T(8,128)(2,1)} %all-gather.4.cloned.1.call-done), kind=kOutput, calls=%fused_computation.50 | convolution fusion | flops 10873405440 | bytes 22413312 | tf_op jit(solution)/shard_map/erf,edf->erd/dot_general | solution.py:125
  692.2 26.9 %copy.97 = bf16[1,2304,768]{2,0,1:T(2,128)(2,1)} copy(bf16[1,2304,768]{2,1,0:T(8,128)(2,1)S(1)} %fusion.39) | data formatting | bytes 7077888 | tf_op jit(solution)/shard_map/convert_element_type | solution.py:250
  719.1 77.0 %reduce.15 = bf16[2304,768]{1,0:T(8,128)(2,1)} reduce(bf16[2304,1,768]{2,1,0:T(2,128)(2,1)} %bitcast.162, bf16[]{:T(256)} %broadcast.596), dimensions={1}, to_apply=%bitcast.155.reduce_sub_computation | reduce | bytes 7077890
  807.2 16.9 %fusion.43 = bf16[1,768,3072]{2,1,0:T(8,128)(2,1)} fusion(bf16[2304,768]{1,0:T(8,128)(2,1)} %bitcast.10, bf16[2304,3072]{1,0:T(8,128)(2,1)} %fusion.7), kind=kOutput, calls=%fused_computation.52 | convolution fusion | flops 10873995264 | bytes 22413312 | tf_op jit(solution)/shard_map/erd,erf->edf/dot_general | solution.py:116
  835.5 48.8 %all-to-all-done.3 = bf16[8,2,110592]{2,1,0:T(2,128)(2,1)} async-done(((bf16[8,2,110592]{2,1,0:T(2,128)(2,1)}), bf16[8,2,110592]{2,1,0:T(2,128)(2,1)}, u32[]{:S(2)}, u32[]{:S(2)}) %all-to-all-start.3) | async-done | bytes 3538976 | tf_op jit(solution)/shard_map/all_to_all | solution.py:251
  884.3 8.1 reshape.692
  897.7 8.3 gather_fusion.1
  911.1 11.3 select_reduce_fusion
  932.2 10.0 fusion.88
  942.3 28.6 %fusion.67 = bf16[576,1,12,64]{0,3,2,1:T(8,128)(2,1)} fusion(f32[12,576,576]{1,2,0:T(8,128)} %fusion.88, f32[12,576,576]{1,2,0:T(8,128)} %get-tuple-element.118, f32[12,576]{1,0:T(8,128)} %log_add_fusion, bf16[576,3,12,64]{0,3,2,1:T(8,128)(2,1)} %bitcast.170), kind=kOutput, calls=%fused_computation.93 | convolution fusion | flops 537484608 | bytes 72728576 | tf_op jit(solution)/shard_map/while/body/eval_jaxpr/hqk,khd->qhd/dot_general | solution.py:86
  970.8 28.5 %fusion.70 = bf16[576,1,12,64]{0,3,2,1:T(8,128)(2,1)} fusion(f32[12,576,576]{1,2,0:T(8,128)} %fusion.88, f32[12,576,576]{1,2,0:T(8,128)} %get-tuple-element.118, f32[12,576]{1,0:T(8,128)} %log_add_fusion, bf16[576,3,12,64]{0,3,2,1:T(8,128)(2,1)} %bitcast.171), kind=kOutput, calls=%fused_computation.94 | convolution fusion | flops 537484608 | bytes 72728576 | tf_op jit(solution)/shard_map/while/body/eval_jaxpr/hqk,qhd->khd/dot_general | solution.py:89
  999.3 9.1 fusion.64
  1026.6 41.0 %all-reduce = (f32[768]{0:T(1024)}, f32[768]{0:T(1024)}, f32[768,8]{0,1:T(8,128)}) all-reduce(f32[768]{0:T(1024)} %get-tuple-element.63, f32[768]{0:T(1024)} %get-tuple-element.61, f32[768,8]{0,1:T(8,128)} %fusion.127), channel_id=1, replica_groups=mesh['dp'=4,'expert'=8] {'dp','expert'}, use_global_device_ids=true, to_apply=%region_28.29 | all-reduce | flops 7680 | bytes 61440 | tf_op jit(solution)/shard_map/psum | solution.py:271
  1078.5 131.2 %all-reduce.4.cloned.1.call-done = (f32[768,2304]{1,0:T(8,128)}, f32[768,768]{1,0:T(8,128)}) async-done(((f32[768,2304]{1,0:T(8,128)}, f32[768,768]{1,0:T(8,128)}), (f32[768,2304]{1,0:T(8,128)}, f32[768,768]{1,0:T(8,128)})) %all-reduce.4.cloned.1.call-update) | async-done | bytes 9437200 | tf_op jit(solution)/shard_map/psum | solution.py:271
  (212 shorter events, 186.1 us)
Async XLA Ops:
  7.2 100.8 %copy-start = (bf16[768,2304]{1,0:T(8,128)(2,1)S(1)}, bf16[768,2304]{1,0:T(8,128)(2,1)}, u32[]{:S(2)}) copy-start(bf16[768,2304]{1,0:T(8,128)(2,1)} %param.19) | copy-start | bytes 10616836
  7.2 248.9 %all-gather.4.cloned.1.call-start = ((), (), s32[]{:S(2)}) async-start(), calls=%async_computation.6 | async-start | bytes 5898240 | tf_op jit(solution)/shard_map/all_gather | solution.py:210
  20.5 92.4 %copy-start.23 = (f32[576]{0:T(1024)}, f32[576]{0:T(1024)S(1)}, u32[]{:S(2)}) copy-start(f32[576]{0:T(1024)S(1)} %broadcast_multiply_fusion.2) | copy-start | bytes 6916
  22.9 90.1 %copy-start.31 = (f32[576]{0:T(1024)}, f32[576]{0:T(1024)S(1)}, u32[]{:S(2)}) copy-start(f32[576]{0:T(1024)S(1)} %fusion.114) | copy-start | bytes 6916
  31.3 73.2 %copy-start.47 = (s32[1152]{0:T(1024)}, s32[1152]{0:T(1024)S(1)}, u32[]{:S(2)}) copy-start(s32[1152]{0:T(1024)S(1)} %get-tuple-element.116) | copy-start | bytes 13828
  138.1 9.7 copy-start.5
  138.1 9.7 copy-start.49
  151.5 7.5 copy-start.43
  165.3 11.0 copy-start.46
  176.3 79.8 %all-to-all-start = ((bf16[8,288,768]{2,1,0:T(8,128)(2,1)}), bf16[8,288,768]{2,1,0:T(8,128)(2,1)}, u32[]{:S(2)}, u32[]{:S(2)}) async-start(bf16[8,288,768]{2,1,0:T(8,128)(2,1)} %bitcast.166), calls=%async_computation | async-start | bytes 7077888 | tf_op jit(solution)/shard_map/all_to_all | solution.py:202
  180.8 102.1 %all-gather.6.cloned.1.call-start = ((), (), s32[]{:S(2)}) async-start(), calls=%async_computation.7 | async-start | bytes 5898240 | tf_op jit(solution)/shard_map/all_gather | solution.py:211
  409.3 6.6 copy-start.39
  409.3 82.9 %all-to-all-start.1 = ((bf16[8,2,110592]{2,1,0:T(2,128)(2,1)}), bf16[8,2,110592]{2,1,0:T(2,128)(2,1)}, u32[]{:S(2)}, u32[]{:S(2)}) async-start(bf16[8,2,110592]{2,1,0:T(2,128)(2,1)} %reshape.689), calls=%async_computation.1 | async-start | bytes 7077888 | tf_op jit(solution)/shard_map/all_to_all | solution.py:214
  413.9 658.8 %reduce-scatter.5.cloned.1.call-start = ((), (), s32[]{:S(2)}) async-start(), calls=%async_computation.9 | async-start | bytes 5898240 | tf_op jit(solution)/shard_map/reduce_scatter | solution.py:246
  416.0 6.8 copy-start.27
  429.4 76.5 %copy-start.20 = (s32[2048]{0:T(1024)}, s32[2048]{0:T(1024)S(1)}, u32[]{:S(2)}) copy-start(s32[2048]{0:T(1024)S(1)} %pad_clamp_fusion) | copy-start | bytes 24580
  431.5 402.4 %copy-start.25 = (f32[576]{0:T(1024)}, f32[576]{0:T(1024)S(1)}, u32[]{:S(2)}) copy-start(f32[576]{0:T(1024)S(1)} %fusion.101) | copy-start | bytes 6916
  514.1 7.2 copy-start.28
  514.1 7.2 copy-start.40
  802.7 81.6 %all-to-all-start.3 = ((bf16[8,2,110592]{2,1,0:T(2,128)(2,1)}), bf16[8,2,110592]{2,1,0:T(2,128)(2,1)}, u32[]{:S(2)}, u32[]{:S(2)}) async-start(bf16[8,2,110592]{2,1,0:T(2,128)(2,1)} %reshape.691), calls=%async_computation.3 | async-start | bytes 7077888 | tf_op jit(solution)/shard_map/all_to_all | solution.py:251
  807.2 268.5 %reduce-scatter.3.cloned.1.call-start = ((), (), s32[]{:S(2)}) async-start(), calls=%async_computation.8 | async-start | bytes 5898240 | tf_op jit(solution)/shard_map/reduce_scatter | solution.py:243
  824.2 385.5 %all-reduce.4.cloned.1.call-start = ((), (), s32[]{:S(2)}) async-start(), calls=%async_computation.10 | async-start | bytes 18874368 | tf_op jit(solution)/shard_map/psum | solution.py:271
  911.1 11.4 copy-start.2
  911.1 11.4 copy-start.19
  911.1 11.4 copy-start.22
  911.1 11.4 copy-start.26
  911.1 11.4 copy-start.30
  999.3 9.1 copy-start.13
  999.3 9.1 copy-start.14
  1020.2 4.9 copy-start.45
  1020.2 48.0 %copy-start.42 = (f32[576]{0:T(1024)S(1)}, f32[576]{0:T(1024)}, u32[]{:S(2)}) copy-start(f32[576]{0:T(1024)} %copy-done.41) | copy-start | bytes 6916
  1209.7 6.6 copy-start.12
  (29 other events, 54.2 us)
Sparse Core Ops, SparseCore 0:
  9.6 40.2 all-gather.3
  183.2 37.8 all-gather.5
  641.0 46.5 reduce-scatter.4
  824.3 49.2 reduce-scatter.2
  1018.3 191.3 all-reduce.3
where the time goes:
time: 1230 us; the launch traced here: 1220 us
  waiting for transfers between devices  316 us (26%)
  matrix products  252 us (20%)
  other arithmetic  235 us (19%)
  local copies, waits for them, and re-layouts  198 us (16%)
  blocking collectives  195 us (16%)
  between operations  14.5 us (1%)
  starting transfers between devices  13.8 us (1%)
    unnamed x4, other arithmetic  157 us
    psum x1, waiting for transfers between devices, local(): lax.psum((jnp.sum(grad_qkv, axis=0), jnp.sum(grad_o, axis=0), grad_w_rout...  131 us
    all_to_all x1, blocking collectives, local(): lax.all_to_all(grad_buffer.reshape(experts, slot_count, features), 'exper...  83.3 us
    all_to_all x1, waiting for transfers between devices, local(): lax.all_to_all(send_buffer.reshape(experts, slot_count, features), 'exper...  74.5 us
    all_gather x1, blocking collectives, local(): lax.all_gather(histogram[None], ('dp', 'expert'), axis=0, tiled=True)  70.5 us
    all_to_all x1, waiting for transfers between devices, local(): lax.all_to_all(result, 'expert', split_axis=1, concat_axis=0, tiled=True)  60.1 us
    unnamed x116, local copies, waits for them, and re-layouts  59.2 us
    all_to_all x1, waiting for transfers between devices, local(): lax.all_to_all(grad_rows, 'expert', split_axis=1, concat_axis=0, tiled=True)  48.8 us
  transfers between devices with their start and end apart: 8, of which 4 were waited for; matrix products, arithmetic and copies ran while one was open for 39% of the time, Pallas kernels for 0%

commit v1 on v0

v1 whole, which is shorter than its diff:
```python
import functools

import jax
import jax.numpy as jnp
from jax import lax
from jax.experimental import pallas as pl
from jax.experimental.pallas import tpu as pltpu
from jax.sharding import PartitionSpec as P

HEADS = 12
HEAD_DIM = 64
LEVELS = 64
BINS = 2 * LEVELS
LIMIT = 60 * 1024 * 1024
F32 = jnp.float32
BF16 = jnp.bfloat16


def dot(a, b, ca=1, cb=0, precision=None):
    return lax.dot_general(
        a, b, (((ca,), (cb,)), ((), ())), precision=precision, preferred_element_type=F32
    )


def whole(shape):
    zeros = (0,) * len(shape)
    return pl.BlockSpec(shape, lambda *_: zeros, pipeline_mode=pl.Buffered(1))


def whole_out(shape):
    zeros = (0,) * len(shape)
    return pl.BlockSpec(shape, lambda *_: zeros)


def iota(shape, dim):
    return lax.broadcasted_iota(jnp.int32, shape, dim)


def call(kernel, grid, ins, in_specs, outs, out_specs, scratch=(), flops=0, moved=0):
    return pl.pallas_call(
        kernel,
        grid=grid,
        in_specs=in_specs,
        out_specs=out_specs,
        out_shape=outs,
        scratch_shapes=list(scratch),
        compiler_params=pltpu.CompilerParams(vmem_limit_bytes=LIMIT),
        cost_estimate=pl.CostEstimate(flops=flops, bytes_accessed=moved, transcendentals=0),
    )(*ins)


def shape_of(shape, dtype):
    return jax.ShapeDtypeStruct(shape, dtype)


def norm_parts(values):
    center = values - jnp.mean(values, axis=-1, keepdims=True)
    spread = jnp.mean(center * center, axis=-1, keepdims=True)
    scale = lax.rsqrt(spread + 1e-06)
    return center * scale, scale


def norm_back(unit, scale, grad_unit):
    return scale * (
        grad_unit
        - jnp.mean(grad_unit, axis=-1, keepdims=True)
        - unit * jnp.mean(grad_unit * unit, axis=-1, keepdims=True)
    )


def class_rows(level_row, which, tokens):
    return (iota((BINS, tokens), 0) == which * LEVELS + (LEVELS - 1) - level_row).astype(F32)


def route_kernel(slots, experts, routes_ref, prio_ref, pad_ref, hist_ref, info_ref):
    tokens = routes_ref.shape[0]
    pair_cols = routes_ref[...].astype(F32)
    pick = (iota((8, 2), 0) == iota((8, 2), 1)).astype(F32)
    rows = dot(pick, pair_cols, 1, 1)
    prio = prio_ref[...]
    valid = (pad_ref[...] > 0).astype(F32)
    early = iota((tokens, tokens), 0) < iota((tokens, tokens), 1)
    hot = [(iota((experts, tokens), 0) == rows[k : k + 1].astype(jnp.int32)).astype(F32) for k in (0, 1)]
    count = dot((hot[0] + hot[1]).astype(BF16), early.astype(BF16))
    hist = jnp.zeros((experts, BINS), F32)
    sides = jnp.where(iota((8, tokens), 0) == 0, prio.astype(F32), valid)
    eye = (iota((8, 8), 0) == iota((8, 8), 1)).astype(F32)
    cols = dot(sides, eye, 0, 0)
    prio_col = cols[:, 0:1]
    valid_col = cols[:, 1:2]
    for k in (0, 1):
        slot = jnp.sum(hot[k] * count, axis=0, keepdims=True)
        info_ref[k : k + 1, :] = rows[k : k + 1]
        info_ref[2 + k : 3 + k, :] = rows[k : k + 1] * slots + slot
        hist = hist + dot(hot[k] * valid, class_rows(prio, k, tokens), 1, 1)
        code_row = rows[k : k + 1] * LEVELS + prio.astype(F32)
        code_col = jnp.where(valid_col > 0, pair_cols[:, k : k + 1] * LEVELS + prio_col, -1.0)
        same = (code_col == code_row) & early
        info_ref[4 + k : 5 + k, :] = jnp.sum(same.astype(F32), axis=0, keepdims=True)
    info_ref[6:7, :] = prio.astype(F32)
    info_ref[7:8, :] = valid
    hist_ref[...] = hist.astype(jnp.int32)


def slot_hot(target_rows, expert, slots, tokens):
    place = iota((slots, tokens), 0) + expert * slots
    return ((place == target_rows[0:1]) | (place == target_rows[1:2])).astype(F32).astype(BF16)


def spread_kernel(slots, info_ref, rows_ref, out_ref):
    target = info_ref[2:4, :].astype(jnp.int32)
    hot = slot_hot(target, pl.program_id(0), slots, rows_ref.shape[0])
    out_ref[0] = dot(hot, rows_ref[...]).astype(BF16)


def keep_kernel(slots, capacity, me_ref, hist_ref, info_ref, rows_ref, out_ref, kept_ref):
    devices, experts, bins = hist_ref.shape
    tokens = rows_ref.shape[0]

    @pl.when(pl.program_id(0) == 0)
    def _():
        def add(j, sums):
            block = hist_ref[j].astype(F32)
            lower = (j < me_ref[0]).astype(F32)
            return sums[0] + block, sums[1] + block * lower

        zero = jnp.zeros((experts, bins), F32)
        totals, before = lax.fori_loop(0, devices, add, (zero, zero))
        early = (iota((bins, bins), 0) < iota((bins, bins), 1)).astype(F32)
        exact = lax.Precision.HIGHEST
        base = dot(totals, early, precision=exact) + before
        prio = info_ref[6:7, :].astype(jnp.int32)
        valid = info_ref[7:8, :] > 0
        for k in (0, 1):
            hot = (iota((experts, tokens), 0) == info_ref[k : k + 1, :].astype(jnp.int32)).astype(F32)
            spot = dot(base, class_rows(prio, k, tokens), precision=exact)
            rank = jnp.sum(hot * spot, axis=0, keepdims=True) + info_ref[4 + k : 5 + k, :]
            kept = valid & (rank < capacity - 0.5)
            kept_ref[k : k + 1, :] = jnp.where(kept, info_ref[2 + k : 3 + k, :].astype(jnp.int32), -1)
        kept_ref[2:8, :] = jnp.full((6, tokens), -1, jnp.int32)

    hot = slot_hot(kept_ref[0:2, :], pl.program_id(0), slots, tokens)
    out_ref[0] = dot(hot, rows_ref[...]).astype(BF16)


def attend_kernel(
    tok_ref, seg_ref, pad_ref, ga_ref, wqkv_ref, wo_ref, gm_ref,
    hidden_ref, normed_ref, proj_ref, mix_ref, prob_ref, nmoe_ref, bias_ref,
):
    step = pl.program_id(0)
    tokens, features = tok_ref.shape

    @pl.when(step == 0)
    def _():
        unit, _ = norm_parts(tok_ref[...].astype(F32))
        normed = (unit * ga_ref[...]).astype(BF16)
        normed_ref[...] = normed
        for part in range(3):
            at = slice(part * features, (part + 1) * features)
            proj_ref[:, at] = dot(normed, wqkv_ref[:, at]).astype(BF16)
        seg = seg_ref[...].astype(F32)
        eye = (iota((8, 8), 0) == iota((8, 8), 1)).astype(F32)
        seg_col = dot(jnp.broadcast_to(seg, (8, tokens)), eye, 0, 0)[:, 0:1]
        own = iota((tokens, tokens), 0) == iota((tokens, tokens), 1)
        allowed = (seg_col == seg) & ((pad_ref[...] > 0) | own)
        bias_ref[...] = jnp.where(allowed, 0.0, -1e30)

    at = lambda part: pl.ds(pl.multiple_of(part * features + step * 128, 128), 128)
    query, keys, value = proj_ref[:, at(0)], proj_ref[:, at(1)], proj_ref[:, at(2)]
    first = iota((tokens, 128), 1) < HEAD_DIM
    mixed = []
    for h in (0, 1):
        mine = first if h == 0 else ~first
        own_query = jnp.where(mine, query.astype(F32) * HEAD_DIM ** (-0.5), 0.0).astype(BF16)
        scores = dot(own_query, keys, 1, 1) + bias_ref[...]
        top = jnp.max(scores, axis=-1, keepdims=True)
        exponent = jnp.exp(scores - top)
        total = jnp.sum(exponent, axis=-1, keepdims=True)
        prob = (exponent * (1.0 / total)).astype(BF16)
        prob_ref[h] = prob
        mixed.append(dot(prob, value))
    mix_ref[:, at(0)] = jnp.where(first, mixed[0], mixed[1]).astype(BF16)

    @pl.when(step == pl.num_programs(0) - 1)
    def _():
        hidden = tok_ref[...].astype(F32) + dot(mix_ref[...], wo_ref[...])
        hidden_ref[...] = hidden
        unit, _ = norm_parts(hidden)
        nmoe_ref[...] = (unit * gm_ref[...]).astype(BF16)


def gather_rows(kept_ref, rows_ref, tokens):
    experts, slots, features = rows_ref.shape

    def add(e, total):
        hot = slot_hot(kept_ref[0:2, :], e, slots, tokens)
        return total + dot(hot, rows_ref[e], 0, 0)

    return lax.fori_loop(0, experts, add, jnp.zeros((tokens, features), F32))


def block_kernel(kept_ref, rows_ref, hidden_ref, out_ref):
    tokens = hidden_ref.shape[0]
    out_ref[...] = (hidden_ref[...] + gather_rows(kept_ref, rows_ref, tokens)).astype(BF16)


def attend_back_kernel(
    kept_ref, rows_ref, hidden_ref, cot_ref, tok_ref, ga_ref, gm_ref, wqkv_ref, wo_ref,
    normed_ref, proj_ref, mix_ref, prob_ref,
    gtok_ref, gqkv_ref, go_ref, gain_ref, dhid_ref, dmix_ref, dproj_ref,
):
    step = pl.program_id(0)
    tokens, features = tok_ref.shape

    @pl.when(step == 0)
    def _():
        grad = gather_rows(kept_ref, rows_ref, tokens)
        unit, scale = norm_parts(hidden_ref[...])
        gain_ref[1:2, :] = jnp.sum(grad * unit, axis=0, keepdims=True)
        dhid = cot_ref[...].astype(F32) + norm_back(unit, scale, grad * gm_ref[...])
        dhid_ref[...] = dhid
        branch = dhid.astype(BF16)
        go_ref[...] = dot(mix_ref[...], branch, 0, 0).astype(BF16)
        dmix_ref[...] = dot(branch, wo_ref[...], 1, 1).astype(BF16)

    at = lambda part: pl.ds(pl.multiple_of(part * features + step * 128, 128), 128)
    query, keys, value = proj_ref[:, at(0)], proj_ref[:, at(1)], proj_ref[:, at(2)]
    dmix = dmix_ref[:, at(0)]
    product = dmix.astype(F32) * mix_ref[:, at(0)].astype(F32)
    first = iota((tokens, 128), 1) < HEAD_DIM
    parts = []
    for h in (0, 1):
        mine = first if h == 0 else ~first
        own_dmix = jnp.where(mine, dmix.astype(F32), 0.0).astype(BF16)
        delta = jnp.sum(jnp.where(mine, product, 0.0), axis=-1, keepdims=True)
        prob = prob_ref[h]
        dprob = dot(own_dmix, value, 1, 1)
        dscore = (prob.astype(F32) * (dprob - delta) * HEAD_DIM ** (-0.5)).astype(BF16)
        parts.append((dot(dscore, keys), dot(dscore, query, 0, 0), dot(prob, dmix, 0, 0)))
    for part in range(3):
        dproj_ref[:, at(part)] = jnp.where(first, parts[0][part], parts[1][part]).astype(BF16)

    @pl.when(step == pl.num_programs(0) - 1)
    def _():
        grad = jnp.zeros((tokens, features), F32)
        for part in range(3):
            cols = slice(part * features, (part + 1) * features)
            gqkv_ref[:, cols] = dot(normed_ref[...], dproj_ref[:, cols], 0, 0).astype(BF16)
            grad = grad + dot(dproj_ref[:, cols], wqkv_ref[:, cols], 1, 1)
        unit, scale = norm_parts(tok_ref[...].astype(F32))
        gain_ref[0:1, :] = jnp.sum(grad * unit, axis=0, keepdims=True)
        gain_ref[2:8, :] = jnp.zeros((6, features), F32)
        gtok_ref[...] = dhid_ref[...] + norm_back(unit, scale, grad * ga_ref[...])


def expert_kernel(pieces, *refs):
    x_ref, g_ref, wr_ref, own_ref = refs[:4]
    win = refs[4 : 4 + pieces]
    wout = refs[4 + pieces : 4 + 2 * pieces]
    y_ref, dx_ref, dexp_ref, gwr_ref = refs[4 + 2 * pieces : 8 + 2 * pieces]
    act = refs[8 + 2 * pieces : 8 + 3 * pieces]
    dpre = refs[8 + 3 * pieces :]
    x = x_ref[0]
    g = g_ref[0].astype(F32)
    logits = dot(x, wr_ref[...])
    exponent = jnp.exp(logits - jnp.max(logits, axis=-1, keepdims=True))
    router = exponent / jnp.sum(exponent, axis=-1, keepdims=True)
    gate = jnp.sum(router * own_ref[...], axis=-1, keepdims=True)
    dexp = (gate * g).astype(BF16)
    dexp_ref[...] = dexp
    out = jnp.zeros(x.shape, F32)
    dx = jnp.zeros(x.shape, F32)
    for r in range(pieces):
        pre = dot(x, win[r][...])
        square = pre * pre
        bend = jnp.tanh(0.7978845608028654 * pre * (1.0 + 0.044715 * square))
        half = 0.5 * (1.0 + bend)
        slope = half + (0.5 * 0.7978845608028654) * pre * (1.0 - bend * bend) * (1.0 + 0.134145 * square)
        active = (pre * half).astype(BF16)
        act[r][...] = active
        dpreact = (dot(dexp, wout[r][...], 1, 1) * slope).astype(BF16)
        dpre[r][...] = dpreact
        out = out + dot(active, wout[r][...])
        dx = dx + dot(dpreact, win[r][...], 1, 1)
    out = out.astype(BF16).astype(F32)
    y_ref[0] = (gate * out).astype(BF16)
    dgate = jnp.sum(g * out, axis=-1, keepdims=True)
    dlogits = (dgate * gate * (own_ref[...] - router)).astype(BF16)
    dx_ref[0] = (dx + dot(dlogits, wr_ref[...], 1, 1)).astype(BF16)

    @pl.when(pl.program_id(0) == 0)
    def _():
        gwr_ref[...] = jnp.zeros(gwr_ref.shape, F32)

    gwr_ref[...] += dot(x, dlogits, 0, 0)


def swap(value, axis, bit):
    size = lax.axis_size(axis)
    return lax.ppermute(value, axis, [(i, i ^ bit) for i in range(size)])


def bits_of(axis):
    size = lax.axis_size(axis)
    return [1 << b for b in range(size.bit_length() - 1)]


def all_sum(value, steps):
    rows = value.shape[0]
    place = []
    for axis, bit in steps:
        half = value.shape[0] // 2
        mine = ((lax.axis_index(axis) & bit) > 0).astype(jnp.int32)
        keep = lax.dynamic_slice_in_dim(value, mine * half, half, 0)
        give = lax.dynamic_slice_in_dim(value, (1 - mine) * half, half, 0)
        value = (keep.astype(F32) + swap(give, axis, bit).astype(F32)).astype(BF16)
        place.append(mine)
    for (axis, bit), mine in zip(reversed(steps), reversed(place)):
        other = swap(value, axis, bit)
        low = jnp.where(mine > 0, other, value)
        high = jnp.where(mine > 0, value, other)
        value = jnp.concatenate([low, high], axis=0)
    return value


def local(
    tokens, segment_ids, pad_mask, routes, priority, gain_attn, w_qkv, w_o, gain_moe, w_router,
    w_in, w_out, cotangent,
):
    sequences, length, features = tokens.shape
    count = sequences * length
    experts = w_router.shape[1]
    groups = lax.axis_size("expert")
    replicas = lax.axis_size("dp")
    devices = groups * replicas
    most = 4 * count // experts
    slots = -(-most // 16) * 16
    capacity = (42 * count * devices + 20 * experts - 1) // (20 * experts)
    me = lax.axis_index(("dp", "expert"))
    tok = tokens.reshape(count, features)
    cot = cotangent.reshape(count, features)
    ga = gain_attn.reshape(1, features)
    gm = gain_moe.reshape(1, features)
    sent = shape_of((experts, slots, features), BF16)
    pair_cost = 2 * experts * slots * count * features

    win, wout = {0: w_in[0]}, {0: w_out[0]}
    for bit in reversed(bits_of("dp")):
        for r in list(win):
            win[r ^ bit] = swap(win[r], "dp", bit)
            wout[r ^ bit] = swap(wout[r], "dp", bit)

    hist, info = call(
        functools.partial(route_kernel, slots, experts),
        (1,),
        (routes.reshape(count, 2), priority.reshape(1, count), pad_mask.reshape(1, count)),
        [whole((count, 2)), whole((1, count)), whole((1, count))],
        (shape_of((experts, BINS), jnp.int32), shape_of((8, count), F32)),
        (whole_out((experts, BINS)), whole_out((8, count))),
        flops=4 * count * count * experts,
    )
    every = lax.all_to_all(
        jnp.broadcast_to(hist[None], (devices, experts, BINS)), ("dp", "expert"), 0, 0, tiled=True
    )
    row_block = pl.BlockSpec((1, slots, features), lambda e: (e, 0, 0))
    g_sent = call(
        functools.partial(spread_kernel, slots),
        (experts,),
        (info, cot),
        [whole((8, count)), whole((count, features))],
        sent,
        row_block,
        flops=pair_cost,
    )
    g_rows = lax.all_to_all(g_sent, "expert", 0, 0, tiled=True)

    pairs = features // 128
    tile = lambda dtype: shape_of((count, features), dtype)
    full = (count, features)
    prob_block = pl.BlockSpec((2, count, count), lambda i: (i, 0, 0))
    hidden, normed, proj, mix, prob, normed_moe = call(
        attend_kernel,
        (pairs,),
        (tok, segment_ids.reshape(1, count), pad_mask.reshape(1, count), ga, w_qkv, w_o, gm),
        [whole(full), whole((1, count)), whole((1, count)), whole((1, features)), whole(w_qkv.shape), whole(w_o.shape), whole((1, features))],
        (tile(F32), tile(BF16), shape_of((count, 3 * features), BF16), tile(BF16), shape_of((HEADS, count, count), BF16), tile(BF16)),
        (whole_out(full), whole_out(full), whole_out((count, 3 * features)), whole_out(full), prob_block, whole_out(full)),
        [pltpu.VMEM((count, count), F32)],
        flops=16 * 10**9,
    )
    x_sent, kept = call(
        functools.partial(keep_kernel, slots, capacity),
        (experts,),
        (me.astype(jnp.int32).reshape(1), every, info, normed_moe),
        [pl.BlockSpec(memory_space=pltpu.SMEM), whole((devices, experts, BINS)), whole((8, count)), whole(full)],
        (sent, shape_of((8, count), jnp.int32)),
        (row_block, whole_out((8, count))),
        flops=pair_cost,
    )
    x_rows = lax.all_to_all(x_sent, "expert", 0, 0, tiled=True)

    hidden_units = w_in.shape[2]
    own = (iota((1, experts), 1) == lax.axis_index("expert")).astype(F32)
    flat = experts * slots
    unit_rows = shape_of((flat, hidden_units), BF16)
    unit_block = pl.BlockSpec((slots, hidden_units), lambda e: (e, 0))
    outs = call(
        functools.partial(expert_kernel, replicas),
        (experts,),
        (x_rows, g_rows, w_router, own, *[win[r] for r in range(replicas)], *[wout[r] for r in range(replicas)]),
        [row_block, row_block, whole(w_router.shape), whole((1, experts))]
        + [whole((features, hidden_units))] * replicas
        + [whole((hidden_units, features))] * replicas,
        (sent, sent, shape_of((flat, features), BF16), shape_of(w_router.shape, F32), *[unit_rows] * (2 * replicas)),
        (row_block, row_block, pl.BlockSpec((slots, features), lambda e: (e, 0)), whole_out(w_router.shape), *[unit_block] * (2 * replicas)),
        flops=8 * flat * features * hidden_units * replicas,
    )
    y_sent, d_sent, dexp, grad_router = outs[:4]
    act, dpre = outs[4 : 4 + replicas], outs[4 + replicas :]
    d_rows = lax.all_to_all(d_sent, "expert", 0, 0, tiled=True)
    y_rows = lax.all_to_all(y_sent, "expert", 0, 0, tiled=True)

    flat_x = x_rows.reshape(flat, features)
    gin = {r: dot(flat_x, dpre[r], 0, 0).astype(BF16) for r in range(replicas)}
    gout = {r: dot(act[r], dexp, 0, 0).astype(BF16) for r in range(replicas)}
    for bit in bits_of("dp"):
        for r in list(gin):
            if r & bit:
                other_in, other_out = swap(gin.pop(r), "dp", bit), swap(gout.pop(r), "dp", bit)
                sum_in = gin[r ^ bit].astype(F32) + other_in.astype(F32)
                sum_out = gout[r ^ bit].astype(F32) + other_out.astype(F32)
                last = len(gin) == 1
                gin[r ^ bit] = sum_in if last else sum_in.astype(BF16)
                gout[r ^ bit] = sum_out if last else sum_out.astype(BF16)

    gtok, gqkv, go, gains = call(
        attend_back_kernel,
        (pairs,),
        (kept, d_rows, hidden, cot, tok, ga, gm, w_qkv, w_o, normed, proj, mix, prob),
        [whole((8, count)), whole((experts, slots, features)), whole(full), whole(full), whole(full), whole((1, features)), whole((1, features)), whole(w_qkv.shape), whole(w_o.shape), whole(full), whole((count, 3 * features)), whole(full), prob_block],
        (tile(F32), shape_of(w_qkv.shape, BF16), shape_of(w_o.shape, BF16), shape_of((8, features), F32)),
        (whole_out(full), whole_out(w_qkv.shape), whole_out(w_o.shape), whole_out((8, features))),
        [pltpu.VMEM(full, F32), pltpu.VMEM(full, BF16), pltpu.VMEM((count, 3 * features), BF16)],
        flops=30 * 10**9,
    )
    block_out = call(
        block_kernel,
        (1,),
        (kept, y_rows, hidden),
        [whole((8, count)), whole((experts, slots, features)), whole(full)],
        tile(BF16),
        whole_out(full),
        flops=pair_cost,
    )
    small = jnp.concatenate(
        [gains[0].reshape(features, 1), gains[1].reshape(features, 1), grad_router], axis=1
    )
    small = jnp.pad(small, ((0, 0), (0, -small.shape[1] % 128))).astype(BF16)
    steps = [("dp", b) for b in bits_of("dp")] + [("expert", b) for b in bits_of("expert")]
    total = all_sum(jnp.concatenate([gqkv, go, small], axis=1), steps).astype(F32)
    edge = 3 * features
    return (
        block_out.reshape(sequences, length, features),
        gtok.reshape(sequences, length, features),
        total[:, edge + features],
        total[:, :edge],
        total[:, edge : edge + features],
        total[:, edge + features + 1],
        total[:, edge + features + 2 : edge + features + 2 + experts],
        gin[0][None],
        gout[0][None],
    )


def solution(mesh):
    rows = P(("dp", "expert"), None, None)
    flat = P(("dp", "expert"), None)
    first = P("expert", None, "dp")
    second = P("expert", "dp", None)
    return jax.shard_map(
        local,
        mesh=mesh,
        in_specs=(rows, flat, flat, rows, flat, P(), P(), P(), P(), P(), first, second, rows),
        out_specs=(rows, rows, P(), P(), P(), P(), P(), first, second),
        check_vma=False,
    )
```

time: 1230 us -> 659 us (0.54)
  matrix products: 252 us -> 27.5 us
  other arithmetic: 235 us -> 24.6 us
  blocking collectives: 195 us -> 0 us
  local copies, waits for them, and re-layouts: 198 us -> 21.3 us
  Pallas kernels: 0 us -> 150 us
  waiting for transfers between devices: 316 us -> 385 us
  starting transfers between devices: 13.8 us -> 42.5 us
  between operations: 14.5 us -> 1.52 us
    ppermute x0 -> x22, waiting for transfers between devices: none -> 235 us  [swap(): return lax.ppermute(value, axis, [(i, i ^ bit) for i in range(size)])]
    dot_general x23 -> x8, matrix products: 252 us -> 27.5 us  [dot(): lax.dot_general(a, b, (((ca,), (cb,)), ((), ())), precision=precision, pr...]
    unnamed x4 -> x0, other arithmetic: 157 us -> none
    pallas_call x0 -> x7, Pallas kernels: none -> 150 us  [call(): pl.pallas_call(kernel, grid=grid, in_specs=in_specs, out_specs=out_specs,...]
    psum x1 -> x0, waiting for transfers between devices: 131 us -> none  [local(): lax.psum((jnp.sum(grad_qkv, axis=0), jnp.sum(grad_o, axis=0), grad_w_rout...]
    all_to_all x1 -> x0, blocking collectives: 83.3 us -> none  [local(): lax.all_to_all(grad_buffer.reshape(experts, slot_count, features), 'exper...]
    convert_element_type x6 -> x0, local copies, waits for them, and re-layouts: 71.4 us -> none  [the longest x1 26.9 us: local(): result = expert_forward(received, full_in, full_out).astype(jnp.bfloat16)]
    all_gather x1 -> x0, blocking collectives: 70.5 us -> none  [local(): lax.all_gather(histogram[None], ('dp', 'expert'), axis=0, tiled=True)]
  transfers between devices with their start and end apart: 8 -> 27, of which waited for: 4 -> 18; matrix products, arithmetic and copies ran while one was open for 39% -> 6% of each run, Pallas kernels for 0% -> 7%
where the time goes in v1:
time: 659 us; the launch traced here: 652 us
  waiting for transfers between devices  385 us (58%)
  Pallas kernels  150 us (23%)
  starting transfers between devices  42.5 us (6%)
  matrix products  27.5 us (4%)
  other arithmetic  24.6 us (4%)
  local copies, waits for them, and re-layouts  21.3 us (3%)
    ppermute x22, waiting for transfers between devices, swap(): return lax.ppermute(value, axis, [(i, i ^ bit) for i in range(size)])  235 us
    pallas_call x7, Pallas kernels, call(): pl.pallas_call(kernel, grid=grid, in_specs=in_specs, out_specs=out_specs,...  150 us
    all_to_all x1, waiting for transfers between devices, local(): d_rows = lax.all_to_all(d_sent, 'expert', 0, 0, tiled=True)  77.6 us
    all_to_all x1, waiting for transfers between devices, local(): g_rows = lax.all_to_all(g_sent, 'expert', 0, 0, tiled=True)  48.2 us
    dot_general x8, matrix products, dot(): lax.dot_general(a, b, (((ca,), (cb,)), ((), ())), precision=precision, pr...  27.5 us
    all_to_all x1, waiting for transfers between devices, local(): x_rows = lax.all_to_all(x_sent, 'expert', 0, 0, tiled=True)  22.8 us
    ppermute x22, starting transfers between devices, swap(): return lax.ppermute(value, axis, [(i, i ^ bit) for i in range(size)])  17.4 us
    unnamed x41, local copies, waits for them, and re-layouts  13.5 us
  transfers between devices with their start and end apart: 27, of which 18 were waited for; matrix products, arithmetic and copies ran while one was open for 6% of the time, Pallas kernels for 7%

profile of v1, /device:TPU:0, one launch (start us, length us, event | category | flops | bytes accessed | tf_op | source)
XLA Modules:
  0.0 652.3 jit_solution(13242298799283450308)
XLA Ops:
  6.0 7.3 %all-to-all-start = ((s32[32,8,128]{2,1,0:T(8,128)}), s32[32,8,128]{2,1,0:T(8,128)S(1)}, u32[]{:S(2)}, u32[]{:S(2)}) async-start(s32[32,8,128]{2,1,0:T(8,128)} %broadcast_in_dim.12), calls=%async_computation | async-start | bytes 262144 | tf_op jit(solution)/shard_map/all_to_all | solution.py:362
  13.3 7.0 %shard_map.199 = bf16[8,288,768]{2,1,0:T(8,128)(2,1)} custom-call(f32[8,576]{1,0:T(8,128)} %get-tuple-element.36.info_ref, bf16[576,768]{1,0:T(8,128)(2,1)} %bitcast.46), custom_call_target="tpu_custom_call" | custom-call | flops 2038431744 | tf_op jit(solution)/shard_map/pallas_call | solution.py:40
  21.7 5.1 all-to-all-start.2
  27.9 22.2 %shard_map.197 = (f32[576,768]{1,0:T(8,128)}, bf16[576,768]{1,0:T(8,128)(2,1)}, bf16[576,2304]{1,0:T(8,128)(2,1)}, bf16[576,768]{1,0:T(8,128)(2,1)}, bf16[12,576...) custom-call(bf16[576,768]{1,0:T(8,128)(2,1)} %bitcast.44, s32[1,576]{1,0:T(1,128)} %seg_ref.1, s32[1,576]{1,0:T(1,128)} %pad_ref.3, ...), custom_call_target="tpu_custom_call" | custom-call | flops 16000000000 | tf_op jit(solution)/shard_map/pallas_call | solution.py:40
  50.1 7.9 %shard_map.198 = (bf16[8,288,768]{2,1,0:T(8,128)(2,1)}, s32[8,576]{1,0:T(8,128)}) custom-call(s32[1]{0:T(128)} %bitcast.me_ref, s32[32,8,128]{2,1,0:T(8,128)} %copy-done.7, f32[8,576]{1,0:T(8,128)} %get-tuple-element.36.info_ref, bf16[576,768]{1,0:T(8,128)(2,1)} %get-tuple-element.37.rows_ref), custom_call_target="tpu_custom_call" | custom-call | flops 2038431744 | tf_op jit(solution)/shard_map/pallas_call | solution.py:40
  58.0 48.2 %all-to-all-done.2.refs_1_ = bf16[8,288,768]{2,1,0:T(8,128)(2,1)S(1)} async-done(((bf16[8,288,768]{2,1,0:T(8,128)(2,1)}), bf16[8,288,768]{2,1,0:T(8,128)(2,1)S(1)}, u32[]{:S(2)}, u32[]{:S(2)}) %all-to-all-start.2) | async-done | bytes 3538976 | tf_op jit(solution)/shard_map/all_to_all | solution.py:375
  107.9 3.9 all-to-all-start.1
  114.4 26.7 %collective-permute-done.1.refs_6_ = bf16[768,768]{1,0:T(8,128)(2,1)} collective-permute-done((bf16[768,768]{1,0:T(8,128)(2,1)}, bf16[768,768]{1,0:T(8,128)(2,1)}, u32[]{:S(2)}, u32[]{:S(2)}) %collective-permute-start.1) | collective-permute-done | bytes 1179680 | tf_op jit(solution)/shard_map/ppermute | solution.py:300
  141.1 24.0 %collective-permute-done.4.refs_10_ = bf16[768,768]{1,0:T(8,128)(2,1)} collective-permute-done((bf16[768,768]{1,0:T(8,128)(2,1)}, bf16[768,768]{1,0:T(8,128)(2,1)}, u32[]{:S(2)}, u32[]{:S(2)}) %collective-permute-start.4) | collective-permute-done | bytes 1179680 | tf_op jit(solution)/shard_map/ppermute | solution.py:300
  168.3 22.8 %all-to-all-done.1.refs_0_ = bf16[8,288,768]{2,1,0:T(8,128)(2,1)S(1)} async-done(((bf16[8,288,768]{2,1,0:T(8,128)(2,1)}), bf16[8,288,768]{2,1,0:T(8,128)(2,1)S(1)}, u32[]{:S(2)}, u32[]{:S(2)}) %all-to-all-start.1) | async-done | bytes 3538976 | tf_op jit(solution)/shard_map/all_to_all | solution.py:400
  192.9 63.7 %shard_map.200 = (bf16[8,288,768]{2,1,0:T(8,128)(2,1)}, bf16[8,288,768]{2,1,0:T(8,128)(2,1)}, bf16[2304,768]{1,0:T(8,128)(2,1)}, f32[768,8]{1,0:T(8,128)}, bf16[...) custom-call(bf16[8,288,768]{2,1,0:T(8,128)(2,1)} %copy-done.3, ...), custom_call_target="tpu_custom_call" | custom-call | flops 43486543872 | tf_op jit(solution)/shard_map/pallas_call | solution.py:40
  256.6 4.1 all-to-all-start.4
  262.4 77.6 %all-to-all-done.4.rows_ref = bf16[8,288,768]{2,1,0:T(8,128)(2,1)S(1)} async-done(((bf16[8,288,768]{2,1,0:T(8,128)(2,1)}), bf16[8,288,768]{2,1,0:T(8,128)(2,1)S(1)}, u32[]{:S(2)}, u32[]{:S(2)}) %all-to-all-start.4) | async-done | bytes 3538976 | tf_op jit(solution)/shard_map/all_to_all | solution.py:420
  341.8 36.0 %shard_map.202 = (f32[576,768]{1,0:T(8,128)}, bf16[768,2304]{1,0:T(8,128)(2,1)}, bf16[768,768]{1,0:T(8,128)(2,1)}, f32[8,768]{1,0:T(8,128)}) custom-call(s32[8,576]{1,0:T(8,128)} %get-tuple-element.38.kept_ref, bf16[8,288,768]{2,1,0:T(8,128)(2,1)} %copy-done.6, f32[576,768]{1,0:T(8,128)} %get-tuple-element.41.hidden_ref, bf16[576,768]{1,0:T(8,128)(2,1)} %bitcast.47, ...), custom_call_target="tpu_custom_call" | custom-call | flops 30000001024 | tf_op jit(solution)/shard_map/pallas_call | solution.py:40
  385.4 4.8 collective-permute-done.6
  395.9 27.9 %collective-permute-done.7 = bf16[192,3200]{1,0:T(8,128)(2,1)} collective-permute-done((bf16[192,3200]{1,0:T(8,128)(2,1)}, bf16[192,3200]{1,0:T(8,128)(2,1)}, u32[]{:S(2)}, u32[]{:S(2)}) %collective-permute-start.7) | collective-permute-done | bytes 1228832 | tf_op jit(solution)/shard_map/ppermute | solution.py:300
  427.9 4.8 all-to-all-start.3
  432.7 28.5 %collective-permute-done.8 = bf16[96,3200]{1,0:T(8,128)(2,1)S(1)} collective-permute-done((bf16[96,3200]{1,0:T(8,128)(2,1)S(1)}, bf16[96,3200]{1,0:T(8,128)(2,1)S(1)}, u32[]{:S(2)}, u32[]{:S(2)}) %collective-permute-start.8) | collective-permute-done | bytes 614432 | tf_op jit(solution)/shard_map/ppermute | solution.py:300
  461.5 6.2 convolution_convert_fusion.4
  467.8 28.6 %collective-permute-done.9 = bf16[48,3200]{1,0:T(8,128)(2,1)S(1)} collective-permute-done((bf16[48,3200]{1,0:T(8,128)(2,1)S(1)}, bf16[48,3200]{1,0:T(8,128)(2,1)S(1)}, u32[]{:S(2)}, u32[]{:S(2)}) %collective-permute-start.9) | collective-permute-done | bytes 307232 | tf_op jit(solution)/shard_map/ppermute | solution.py:300
  496.5 3.9 collective-permute-start.10
  503.5 14.1 %collective-permute-done.10 = bf16[24,3200]{1,0:T(8,128)(2,1)S(1)} collective-permute-done((bf16[24,3200]{1,0:T(8,128)(2,1)S(1)}, bf16[24,3200]{1,0:T(8,128)(2,1)S(1)}, u32[]{:S(2)}, u32[]{:S(2)}) %collective-permute-start.10) | collective-permute-done | bytes 153632 | tf_op jit(solution)/shard_map/ppermute | solution.py:300
  520.9 5.2 collective-permute-done.11
  529.5 4.4 collective-permute-done.12
  534.1 3.6 collective-permute-start.13
  540.7 10.2 %collective-permute-done.13 = bf16[96,3200]{1,0:T(8,128)(2,1)S(1)} collective-permute-done((bf16[96,3200]{1,0:T(8,128)(2,1)S(1)}, bf16[96,3200]{1,0:T(8,128)(2,1)S(1)}, u32[]{:S(2)}, u32[]{:S(2)}) %collective-permute-start.13) | collective-permute-done | bytes 614432 | tf_op jit(solution)/shard_map/ppermute | solution.py:300
  558.5 22.7 %collective-permute-done.14 = bf16[192,3200]{1,0:T(8,128)(2,1)S(1)} collective-permute-done((bf16[192,3200]{1,0:T(8,128)(2,1)S(1)}, bf16[192,3200]{1,0:T(8,128)(2,1)S(1)}, u32[]{:S(2)}, u32[]{:S(2)}) %collective-permute-start.14) | collective-permute-done | bytes 1228832 | tf_op jit(solution)/shard_map/ppermute | solution.py:300
  587.5 3.3 convolution_convert_fusion.3
  590.8 15.6 %collective-permute-done.18 = bf16[768,768]{1,0:T(8,128)(2,1)S(1)} collective-permute-done((bf16[768,768]{1,0:T(8,128)(2,1)S(1)}, bf16[768,768]{1,0:T(8,128)(2,1)S(1)}, u32[]{:S(2)}, u32[]{:S(2)}) %collective-permute-start.18) | collective-permute-done | bytes 1179680 | tf_op jit(solution)/shard_map/ppermute | solution.py:300
  608.4 20.8 %collective-permute-done.21 = bf16[768,768]{1,0:T(8,128)(2,1)S(1)} collective-permute-done((bf16[768,768]{1,0:T(8,128)(2,1)S(1)}, bf16[768,768]{1,0:T(8,128)(2,1)S(1)}, u32[]{:S(2)}, u32[]{:S(2)}) %collective-permute-start.21) | collective-permute-done | bytes 1179680 | tf_op jit(solution)/shard_map/ppermute | solution.py:300
  631.0 10.8 %shard_map.201 = bf16[576,768]{1,0:T(8,128)(2,1)} custom-call(s32[8,576]{1,0:T(8,128)} %get-tuple-element.38.kept_ref, bf16[8,288,768]{2,1,0:T(8,128)(2,1)} %all-to-all-done.3.rows_ref, f32[576,768]{1,0:T(8,128)} %get-tuple-element.41.hidden_ref), custom_call_target="tpu_custom_call" | custom-call | flops 2038431744 | tf_op jit(solution)/shard_map/pallas_call | solution.py:40
  647.6 3.5 slice.32
  (117 shorter events, 75.4 us)
Async XLA Ops:
  6.0 15.0 %all-to-all-start = ((s32[32,8,128]{2,1,0:T(8,128)}), s32[32,8,128]{2,1,0:T(8,128)S(1)}, u32[]{:S(2)}, u32[]{:S(2)}) async-start(s32[32,8,128]{2,1,0:T(8,128)} %broadcast_in_dim.12), calls=%async_computation | async-start | bytes 262144 | tf_op jit(solution)/shard_map/all_to_all | solution.py:362
  21.7 84.5 %all-to-all-start.2 = ((bf16[8,288,768]{2,1,0:T(8,128)(2,1)}), bf16[8,288,768]{2,1,0:T(8,128)(2,1)S(1)}, u32[]{:S(2)}, u32[]{:S(2)}) async-start(bf16[8,288,768]{2,1,0:T(8,128)(2,1)} %shard_map.199), calls=%async_computation.2 | async-start | bytes 7077888 | tf_op jit(solution)/shard_map/all_to_all | solution.py:375
  106.2 58.9 %copy-start.8 = (bf16[768,8]{0,1:T(8,128)(2,1)S(1)}, bf16[768,8]{0,1:T(8,128)(2,1)}, u32[]{:S(2)}) copy-start(bf16[768,8]{0,1:T(8,128)(2,1)} %param.22) | copy-start | bytes 36868
  107.9 83.1 %all-to-all-start.1 = ((bf16[8,288,768]{2,1,0:T(8,128)(2,1)}), bf16[8,288,768]{2,1,0:T(8,128)(2,1)S(1)}, u32[]{:S(2)}, u32[]{:S(2)}) async-start(bf16[8,288,768]{2,1,0:T(8,128)(2,1)} %get-tuple-element.39), calls=%async_computation.1 | async-start | bytes 7077888 | tf_op jit(solution)/shard_map/all_to_all | solution.py:400
  111.8 29.3 %collective-permute-start.1 = (bf16[768,768]{1,0:T(8,128)(2,1)}, bf16[768,768]{1,0:T(8,128)(2,1)}, u32[]{:S(2)}, u32[]{:S(2)}) collective-permute-start(bf16[768,768]{1,0:T(8,128)(2,1)} %bitcast.38), channel_id=1, source_target_pairs={{0,16},{8,24},{16,0},{24,8},{1,17},{9,25},{17,1},{25,9},{2,18},{10... | collective-permute-start | bytes 3538952 | tf_op jit(solution)/shard_map/ppermute | solution.py:300
  113.4 51.7 %collective-permute-start.4 = (bf16[768,768]{1,0:T(8,128)(2,1)}, bf16[768,768]{1,0:T(8,128)(2,1)}, u32[]{:S(2)}, u32[]{:S(2)}) collective-permute-start(bf16[768,768]{1,0:T(8,128)(2,1)} %bitcast.41), channel_id=1, source_target_pairs={{0,16},{8,24},{16,0},{24,8},{1,17},{9,25},{17,1},{25,9},{2,18},{10... | collective-permute-start | bytes 3538952 | tf_op jit(solution)/shard_map/ppermute | solution.py:300
  113.9 52.5 %collective-permute-start = (bf16[768,768]{1,0:T(8,128)(2,1)}, bf16[768,768]{1,0:T(8,128)(2,1)}, u32[]{:S(2)}, u32[]{:S(2)}) collective-permute-start(bf16[768,768]{1,0:T(8,128)(2,1)} %bitcast.39), channel_id=1, source_target_pairs={{0,8},{8,0},{16,24},{24,16},{1,9},{9,1},{17,25},{25,17},{2,10},{10... | collective-permute-start | bytes 3538952 | tf_op jit(solution)/shard_map/ppermute | solution.py:300
  113.9 52.5 %collective-permute-start.3 = (bf16[768,768]{1,0:T(8,128)(2,1)}, bf16[768,768]{1,0:T(8,128)(2,1)}, u32[]{:S(2)}, u32[]{:S(2)}) collective-permute-start(bf16[768,768]{1,0:T(8,128)(2,1)} %bitcast.42), channel_id=1, source_target_pairs={{0,8},{8,0},{16,24},{24,16},{1,9},{9,1},{17,25},{25,17},{2,10},{10... | collective-permute-start | bytes 3538952 | tf_op jit(solution)/shard_map/ppermute | solution.py:300
  141.1 25.4 %collective-permute-start.2 = (bf16[768,768]{1,0:T(8,128)(2,1)}, bf16[768,768]{1,0:T(8,128)(2,1)}, u32[]{:S(2)}, u32[]{:S(2)}) collective-permute-start(bf16[768,768]{1,0:T(8,128)(2,1)} %collective-permute-done.1.refs_6_), channel_id=1, source_target_pairs={{0,8},{8,0},{16,24},{24,16},{1,9},{9,1},{17,25},{25,17},{2,10},{10... | collective-permute-start | bytes 3538952 | tf_op jit(solution)/shard_map/ppermute | solution.py:300
  165.1 3.2 collective-permute-start.5
  256.6 83.4 %all-to-all-start.4 = ((bf16[8,288,768]{2,1,0:T(8,128)(2,1)}), bf16[8,288,768]{2,1,0:T(8,128)(2,1)S(1)}, u32[]{:S(2)}, u32[]{:S(2)}) async-start(bf16[8,288,768]{2,1,0:T(8,128)(2,1)} %get-tuple-element.42), calls=%async_computation.4 | async-start | bytes 7077888 | tf_op jit(solution)/shard_map/all_to_all | solution.py:420
  385.4 4.8 collective-permute-start.6
  394.4 29.4 %collective-permute-start.7 = (bf16[192,3200]{1,0:T(8,128)(2,1)}, bf16[192,3200]{1,0:T(8,128)(2,1)}, u32[]{:S(2)}, u32[]{:S(2)}) collective-permute-start(bf16[192,3200]{1,0:T(8,128)(2,1)} %constant_dynamic-slice_fusion.3), channel_id=1, source_target_pairs={{0,16},{8,24},{16,0},{24,8},{1,17},{9,25},{17,1},{25,9},{2,18},{10... | collective-permute-start | bytes 3686408 | tf_op jit(solution)/shard_map/ppermute | solution.py:300
  426.4 34.8 %collective-permute-start.8 = (bf16[96,3200]{1,0:T(8,128)(2,1)S(1)}, bf16[96,3200]{1,0:T(8,128)(2,1)S(1)}, u32[]{:S(2)}, u32[]{:S(2)}) collective-permute-start(bf16[96,3200]{1,0:T(8,128)(2,1)S(1)} %constant_dynamic-slice_fusion.2), channel_id=1, source_target_pairs={{0,1},{1,0},{2,3},{3,2},{4,5},{5,4},{6,7},{7,6},{8,9},{9,8},{10,11... | collective-permute-start | bytes 1843208 | tf_op jit(solution)/shard_map/ppermute | solution.py:300
  427.9 33.3 %copy-start.2 = (bf16[192,3200]{1,0:T(8,128)(2,1)S(1)}, bf16[192,3200]{1,0:T(8,128)(2,1)}, u32[]{:S(2)}) copy-start(bf16[192,3200]{1,0:T(8,128)(2,1)} %copy-done.1) | copy-start | bytes 3686404
  427.9 203.1 %all-to-all-start.3 = ((bf16[8,288,768]{2,1,0:T(8,128)(2,1)}), bf16[8,288,768]{2,1,0:T(8,128)(2,1)}, u32[]{:S(2)}, u32[]{:S(2)}) async-start(bf16[8,288,768]{2,1,0:T(8,128)(2,1)} %get-tuple-element.40), calls=%async_computation.3 | async-start | bytes 7077888 | tf_op jit(solution)/shard_map/all_to_all | solution.py:421
  461.4 35.0 %collective-permute-start.9 = (bf16[48,3200]{1,0:T(8,128)(2,1)S(1)}, bf16[48,3200]{1,0:T(8,128)(2,1)S(1)}, u32[]{:S(2)}, u32[]{:S(2)}) collective-permute-start(bf16[48,3200]{1,0:T(8,128)(2,1)S(1)} %constant_dynamic-slice_fusion.1), channel_id=1, source_target_pairs={{0,2},{1,3},{2,0},{3,1},{4,6},{5,7},{6,4},{7,5},{8,10},{9,11},{10,... | collective-permute-start | bytes 921608 | tf_op jit(solution)/shard_map/ppermute | solution.py:300
  461.5 38.9 %copy-start.4 = (bf16[8,288,768]{2,1,0:T(8,128)(2,1)S(1)}, bf16[8,288,768]{2,1,0:T(8,128)(2,1)}, u32[]{:S(2)}) copy-start(bf16[8,288,768]{2,1,0:T(8,128)(2,1)} %copy-done.3) | copy-start | bytes 10616836
  461.5 38.9 %copy-start.18 = (bf16[2304,768]{1,0:T(8,128)(2,1)S(1)}, bf16[2304,768]{1,0:T(8,128)(2,1)}, u32[]{:S(2)}) copy-start(bf16[2304,768]{1,0:T(8,128)(2,1)} %get-tuple-element.53) | copy-start | bytes 10616836
  467.7 88.0 %collective-permute-start.17 = (bf16[768,768]{1,0:T(8,128)(2,1)S(1)}, bf16[768,768]{1,0:T(8,128)(2,1)S(1)}, u32[]{:S(2)}, u32[]{:S(2)}) collective-permute-start(bf16[768,768]{1,0:T(8,128)(2,1)S(1)} %convolution_convert_fusion.4), channel_id=1, source_target_pairs={{0,8},{8,0},{16,24},{24,16},{1,9},{9,1},{17,25},{25,17},{2,10},{10... | collective-permute-start | bytes 3538952 | tf_op jit(solution)/shard_map/ppermute | solution.py:300
  496.5 21.1 %collective-permute-start.10 = (bf16[24,3200]{1,0:T(8,128)(2,1)S(1)}, bf16[24,3200]{1,0:T(8,128)(2,1)S(1)}, u32[]{:S(2)}, u32[]{:S(2)}) collective-permute-start(bf16[24,3200]{1,0:T(8,128)(2,1)S(1)} %constant_dynamic-slice_fusion), channel_id=1, source_target_pairs={{0,4},{1,5},{2,6},{3,7},{4,0},{5,1},{6,2},{7,3},{8,12},{9,13},{10,... | collective-permute-start | bytes 460808 | tf_op jit(solution)/shard_map/ppermute | solution.py:300
  500.5 17.3 %copy-start.17 = (bf16[2304,768]{1,0:T(8,128)(2,1)S(1)}, bf16[2304,768]{1,0:T(8,128)(2,1)}, u32[]{:S(2)}) copy-start(bf16[2304,768]{1,0:T(8,128)(2,1)} %get-tuple-element.60) | copy-start | bytes 10616836
  503.4 87.4 %collective-permute-start.16 = (bf16[768,768]{1,0:T(8,128)(2,1)S(1)}, bf16[768,768]{1,0:T(8,128)(2,1)S(1)}, u32[]{:S(2)}, u32[]{:S(2)}) collective-permute-start(bf16[768,768]{1,0:T(8,128)(2,1)S(1)} %convolution_convert_fusion.6), channel_id=1, source_target_pairs={{0,8},{8,0},{16,24},{24,16},{1,9},{9,1},{17,25},{25,17},{2,10},{10... | collective-permute-start | bytes 3538952 | tf_op jit(solution)/shard_map/ppermute | solution.py:300
  517.7 8.4 %collective-permute-start.11 = (bf16[24,3200]{1,0:T(8,128)(2,1)S(1)}, bf16[24,3200]{1,0:T(8,128)(2,1)S(1)}, u32[]{:S(2)}, u32[]{:S(2)}) collective-permute-start(bf16[24,3200]{1,0:T(8,128)(2,1)S(1)} %add_convert_fusion.8), channel_id=1, source_target_pairs={{0,4},{1,5},{2,6},{3,7},{4,0},{5,1},{6,2},{7,3},{8,12},{9,13},{10,... | collective-permute-start | bytes 460808 | tf_op jit(solution)/shard_map/ppermute | solution.py:300
  520.8 35.8 %collective-permute-start.20 = (bf16[768,768]{1,0:T(8,128)(2,1)S(1)}, bf16[768,768]{1,0:T(8,128)(2,1)S(1)}, u32[]{:S(2)}, u32[]{:S(2)}) collective-permute-start(bf16[768,768]{1,0:T(8,128)(2,1)S(1)} %convolution_convert_fusion), channel_id=1, source_target_pairs={{0,8},{8,0},{16,24},{24,16},{1,9},{9,1},{17,25},{25,17},{2,10},{10... | collective-permute-start | bytes 3538952 | tf_op jit(solution)/shard_map/ppermute | solution.py:300
  526.2 7.8 %collective-permute-start.12 = (bf16[48,3200]{1,0:T(8,128)(2,1)S(1)}, bf16[48,3200]{1,0:T(8,128)(2,1)S(1)}, u32[]{:S(2)}, u32[]{:S(2)}) collective-permute-start(bf16[48,3200]{1,0:T(8,128)(2,1)S(1)} %pad_maximum_fusion.4), channel_id=1, source_target_pairs={{0,2},{1,3},{2,0},{3,1},{4,6},{5,7},{6,4},{7,5},{8,10},{9,11},{10,... | collective-permute-start | bytes 921608 | tf_op jit(solution)/shard_map/ppermute | solution.py:300
  529.5 78.9 %collective-permute-start.19 = (bf16[768,768]{1,0:T(8,128)(2,1)S(1)}, bf16[768,768]{1,0:T(8,128)(2,1)S(1)}, u32[]{:S(2)}, u32[]{:S(2)}) collective-permute-start(bf16[768,768]{1,0:T(8,128)(2,1)S(1)} %convolution_convert_fusion.2), channel_id=1, source_target_pairs={{0,8},{8,0},{16,24},{24,16},{1,9},{9,1},{17,25},{25,17},{2,10},{10... | collective-permute-start | bytes 3538952 | tf_op jit(solution)/shard_map/ppermute | solution.py:300
  534.1 16.8 %collective-permute-start.13 = (bf16[96,3200]{1,0:T(8,128)(2,1)S(1)}, bf16[96,3200]{1,0:T(8,128)(2,1)S(1)}, u32[]{:S(2)}, u32[]{:S(2)}) collective-permute-start(bf16[96,3200]{1,0:T(8,128)(2,1)S(1)} %pad_maximum_fusion.3), channel_id=1, source_target_pairs={{0,1},{1,0},{2,3},{3,2},{4,5},{5,4},{6,7},{7,6},{8,9},{9,8},{10,11... | collective-permute-start | bytes 1843208 | tf_op jit(solution)/shard_map/ppermute | solution.py:300
  551.2 30.0 %collective-permute-start.14 = (bf16[192,3200]{1,0:T(8,128)(2,1)S(1)}, bf16[192,3200]{1,0:T(8,128)(2,1)S(1)}, u32[]{:S(2)}, u32[]{:S(2)}) collective-permute-start(bf16[192,3200]{1,0:T(8,128)(2,1)S(1)} %pad_maximum_fusion.2), channel_id=1, source_target_pairs={{0,16},{8,24},{16,0},{24,8},{1,17},{9,25},{17,1},{25,9},{2,18},{10... | collective-permute-start | bytes 3686408 | tf_op jit(solution)/shard_map/ppermute | solution.py:300
  556.0 50.5 %collective-permute-start.18 = (bf16[768,768]{1,0:T(8,128)(2,1)S(1)}, bf16[768,768]{1,0:T(8,128)(2,1)S(1)}, u32[]{:S(2)}, u32[]{:S(2)}) collective-permute-start(bf16[768,768]{1,0:T(8,128)(2,1)S(1)} %add_convert_fusion.4), channel_id=1, source_target_pairs={{0,16},{8,24},{16,0},{24,8},{1,17},{9,25},{17,1},{25,9},{2,18},{10... | collective-permute-start | bytes 3538952 | tf_op jit(solution)/shard_map/ppermute | solution.py:300
  556.9 72.4 %collective-permute-start.21 = (bf16[768,768]{1,0:T(8,128)(2,1)S(1)}, bf16[768,768]{1,0:T(8,128)(2,1)S(1)}, u32[]{:S(2)}, u32[]{:S(2)}) collective-permute-start(bf16[768,768]{1,0:T(8,128)(2,1)S(1)} %add_convert_fusion.2), channel_id=1, source_target_pairs={{0,16},{8,24},{16,0},{24,8},{1,17},{9,25},{17,1},{25,9},{2,18},{10... | collective-permute-start | bytes 3538952 | tf_op jit(solution)/shard_map/ppermute | solution.py:300
  583.3 58.6 %collective-permute-start.15 = (bf16[384,3200]{1,0:T(8,128)(2,1)}, bf16[384,3200]{1,0:T(8,128)(2,1)}, u32[]{:S(2)}, u32[]{:S(2)}) collective-permute-start(bf16[384,3200]{1,0:T(8,128)(2,1)} %pad_maximum_fusion.1), channel_id=1, source_target_pairs={{0,8},{8,0},{16,24},{24,16},{1,9},{9,1},{17,25},{25,17},{2,10},{10... | collective-permute-start | bytes 7372808 | tf_op jit(solution)/shard_map/ppermute | solution.py:300
  (14 other events, 78.0 us)

commit v2 on v1

v2 whole, which is shorter than its diff:
```python
import functools

import jax
import jax.numpy as jnp
from jax import lax
from jax.experimental import pallas as pl
from jax.experimental.pallas import tpu as pltpu
from jax.sharding import PartitionSpec as P

HEADS = 12
HEAD_DIM = 64
LEVELS = 64
BINS = 2 * LEVELS
LIMIT = 60 * 1024 * 1024
F32 = jnp.float32
BF16 = jnp.bfloat16


def dot(a, b, ca=1, cb=0, precision=None):
    return lax.dot_general(
        a, b, (((ca,), (cb,)), ((), ())), precision=precision, preferred_element_type=F32
    )


def whole(shape):
    zeros = (0,) * len(shape)
    return pl.BlockSpec(shape, lambda *_: zeros, pipeline_mode=pl.Buffered(1))


def whole_out(shape):
    zeros = (0,) * len(shape)
    return pl.BlockSpec(shape, lambda *_: zeros)


def iota(shape, dim):
    return lax.broadcasted_iota(jnp.int32, shape, dim)


def call(kernel, grid, ins, in_specs, outs, out_specs, scratch=(), us=1, after=(), alias=()):
    late = len(after)

    def body(*refs):
        kernel(*refs[late:])

    return pl.pallas_call(
        body,
        grid=grid,
        in_specs=[pl.BlockSpec(memory_space=pl.ANY)] * late + in_specs,
        out_specs=out_specs,
        out_shape=outs,
        scratch_shapes=list(scratch),
        input_output_aliases={late + i: o for i, o in alias},
        compiler_params=pltpu.CompilerParams(vmem_limit_bytes=LIMIT),
        cost_estimate=pl.CostEstimate(flops=us * 10**6, bytes_accessed=0, transcendentals=0),
    )(*after, *ins)


def shape_of(shape, dtype):
    return jax.ShapeDtypeStruct(shape, dtype)


def norm_parts(values):
    center = values - jnp.mean(values, axis=-1, keepdims=True)
    spread = jnp.mean(center * center, axis=-1, keepdims=True)
    scale = lax.rsqrt(spread + 1e-06)
    return center * scale, scale


def norm_back(unit, scale, grad_unit):
    return scale * (
        grad_unit
        - jnp.mean(grad_unit, axis=-1, keepdims=True)
        - unit * jnp.mean(grad_unit * unit, axis=-1, keepdims=True)
    )


def class_rows(level_row, which, tokens):
    return (iota((BINS, tokens), 0) == which * LEVELS + (LEVELS - 1) - level_row).astype(F32)


def route_kernel(slots, experts, routes_ref, prio_ref, pad_ref, hist_ref, info_ref, target_ref):
    tokens = routes_ref.shape[0]
    pair_cols = routes_ref[...].astype(F32)
    pick = (iota((8, 2), 0) == iota((8, 2), 1)).astype(F32)
    rows = dot(pick, pair_cols, 1, 1)
    prio = prio_ref[...]
    valid = (pad_ref[...] > 0).astype(F32)
    early = iota((tokens, tokens), 0) < iota((tokens, tokens), 1)
    hot = [(iota((experts, tokens), 0) == rows[k : k + 1].astype(jnp.int32)).astype(F32) for k in (0, 1)]
    count = dot((hot[0] + hot[1]).astype(BF16), early.astype(BF16))
    hist = jnp.zeros((experts, BINS), F32)
    sides = jnp.where(iota((8, tokens), 0) == 0, prio.astype(F32), valid)
    eye = (iota((8, 8), 0) == iota((8, 8), 1)).astype(F32)
    cols = dot(sides, eye, 0, 0)
    prio_col = cols[:, 0:1]
    valid_col = cols[:, 1:2]
    for k in (0, 1):
        slot = jnp.sum(hot[k] * count, axis=0, keepdims=True)
        info_ref[k : k + 1, :] = rows[k : k + 1]
        info_ref[2 + k : 3 + k, :] = rows[k : k + 1] * slots + slot
        hist = hist + dot(hot[k] * valid, class_rows(prio, k, tokens), 1, 1)
        code_row = rows[k : k + 1] * LEVELS + prio.astype(F32)
        code_col = jnp.where(valid_col > 0, pair_cols[:, k : k + 1] * LEVELS + prio_col, -1.0)
        same = (code_col == code_row) & early
        info_ref[4 + k : 5 + k, :] = jnp.sum(same.astype(F32), axis=0, keepdims=True)
    info_ref[6:7, :] = prio.astype(F32)
    info_ref[7:8, :] = valid
    target_ref[...] = jnp.full(target_ref.shape, -1, jnp.int32)
    target_ref[0:2, :] = info_ref[2:4, :].astype(jnp.int32)
    hist_ref[...] = hist.astype(jnp.int32)


def slot_hot(target_rows, expert, slots, tokens):
    place = iota((slots, tokens), 0) + expert * slots
    return ((place == target_rows[0:1]) | (place == target_rows[1:2])).astype(F32).astype(BF16)


def spread_kernel(slots, spot_ref, target_ref, rows_ref, *out_refs):
    for j, out_ref in enumerate(out_refs):
        hot = slot_hot(target_ref[0:2, :], spot_ref[0] ^ j, slots, rows_ref.shape[0])
        out_ref[...] = dot(hot, rows_ref[...]).astype(BF16)


def spread_joint_kernel(slots, spot_ref, targetx_ref, targetg_ref, x_ref, g_ref, out_ref):
    expert, tokens = spot_ref[3] + pl.program_id(0), x_ref.shape[0]
    out_ref[0, :slots] = dot(slot_hot(targetx_ref[0:2, :], expert, slots, tokens), x_ref[...]).astype(BF16)
    out_ref[0, slots:] = dot(slot_hot(targetg_ref[0:2, :], expert, slots, tokens), g_ref[...]).astype(BF16)


def keep_kernel(
    capacity, me_ref, hist_ref, info_ref, target_ref, tok_ref, mix_ref, wo_ref, gm_ref,
    kept_ref, hidden_ref, nmoe_ref,
):
    devices, experts, bins = hist_ref.shape
    tokens = info_ref.shape[1]

    def add(j, sums):
        block = hist_ref[j].astype(F32)
        lower = (j < me_ref[0]).astype(F32)
        return sums[0] + block, sums[1] + block * lower

    zero = jnp.zeros((experts, bins), F32)
    totals, before = lax.fori_loop(0, devices, add, (zero, zero))
    early = (iota((bins, bins), 0) < iota((bins, bins), 1)).astype(F32)
    exact = lax.Precision.HIGHEST
    base = dot(totals, early, precision=exact) + before
    prio = info_ref[6:7, :].astype(jnp.int32)
    valid = info_ref[7:8, :] > 0
    kept_ref[...] = jnp.full(kept_ref.shape, -1, jnp.int32)
    for k in (0, 1):
        hot = (iota((experts, tokens), 0) == info_ref[k : k + 1, :].astype(jnp.int32)).astype(F32)
        spot = dot(base, class_rows(prio, k, tokens), precision=exact)
        rank = jnp.sum(hot * spot, axis=0, keepdims=True) + info_ref[4 + k : 5 + k, :]
        kept = valid & (rank < capacity - 0.5)
        kept_ref[k : k + 1, :] = jnp.where(kept, target_ref[k : k + 1, :], -1)
    hidden = tok_ref[...].astype(F32) + dot(mix_ref[...], wo_ref[...])
    hidden_ref[...] = hidden
    unit, _ = norm_parts(hidden)
    nmoe_ref[...] = (unit * gm_ref[...]).astype(BF16)


def attend_kernel(
    tok_ref, seg_ref, pad_ref, ga_ref, wqkv_ref, normed_ref, proj_ref, mix_ref, prob_ref, bias_ref,
):
    step = pl.program_id(0)
    tokens, features = tok_ref.shape

    @pl.when(step == 0)
    def _():
        unit, _ = norm_parts(tok_ref[...].astype(F32))
        normed = (unit * ga_ref[...]).astype(BF16)
        normed_ref[...] = normed
        for part in range(3):
            at = slice(part * features, (part + 1) * features)
            proj_ref[:, at] = dot(normed, wqkv_ref[:, at]).astype(BF16)
        seg = seg_ref[...].astype(F32)
        eye = (iota((8, 8), 0) == iota((8, 8), 1)).astype(F32)
        seg_col = dot(jnp.broadcast_to(seg, (8, tokens)), eye, 0, 0)[:, 0:1]
        own = iota((tokens, tokens), 0) == iota((tokens, tokens), 1)
        allowed = (seg_col == seg) & ((pad_ref[...] > 0) | own)
        bias_ref[...] = jnp.where(allowed, 0.0, -1e30)

    at = lambda part: pl.ds(pl.multiple_of(part * features + step * 128, 128), 128)
    query, keys, value = proj_ref[:, at(0)], proj_ref[:, at(1)], proj_ref[:, at(2)]
    first = iota((tokens, 128), 1) < HEAD_DIM
    mixed = []
    for h in (0, 1):
        mine = first if h == 0 else ~first
        own_query = jnp.where(mine, query.astype(F32) * HEAD_DIM ** (-0.5), 0.0).astype(BF16)
        scores = dot(own_query, keys, 1, 1) + bias_ref[...]
        top = jnp.max(scores, axis=-1, keepdims=True)
        exponent = jnp.exp(scores - top)
        total = jnp.sum(exponent, axis=-1, keepdims=True)
        prob = (exponent * (1.0 / total)).astype(BF16)
        prob_ref[h] = prob
        mixed.append(dot(prob, value))
    mix_ref[:, at(0)] = jnp.where(first, mixed[0], mixed[1]).astype(BF16)


def gather_rows(spot_ref, kept_ref, rows_refs):
    slots, features = rows_refs[0].shape
    tokens = kept_ref.shape[1]
    total = jnp.zeros((tokens, features), F32)
    for j, rows_ref in enumerate(rows_refs):
        hot = slot_hot(kept_ref[0:2, :], spot_ref[0] ^ j, slots, tokens)
        total = total + dot(hot, rows_ref[...], 0, 0)
    return total


def near_kernel(spot_ref, kept_ref, hidden_ref, *refs):
    d_ref, block_ref = refs[-2:]
    slots, tokens = refs[0].shape[0] // 2, kept_ref.shape[1]
    d_total = jnp.zeros(d_ref.shape, F32)
    y_total = hidden_ref[...]
    for j, rows_ref in enumerate(refs[:-2]):
        hot = slot_hot(kept_ref[0:2, :], spot_ref[0] ^ j, slots, tokens)
        d_total = d_total + dot(hot, rows_ref[:slots, :], 0, 0)
        y_total = y_total + dot(hot, rows_ref[slots:, :], 0, 0)
    d_ref[...] = d_total
    block_ref[...] = y_total


def gather_kernel(spot_ref, kept_ref, *refs):
    refs[-1][...] = gather_rows(spot_ref, kept_ref, refs[:-1]).astype(BF16)


def block_kernel(block_ref, far_ref, out_ref):
    out_ref[...] = (block_ref[...] + far_ref[...].astype(F32)).astype(BF16)


def left_grad_kernel(rows_ref, grad_ref, out_ref):
    out_ref[...] = dot(rows_ref[...], grad_ref[...], 0, 0).astype(BF16)


def right_grad_kernel(rows_ref, grad_ref, _, out_ref, __):
    out_ref[...] = dot(rows_ref[...], grad_ref[...], 0, 0).astype(BF16)


def halves_by(bit, value):
    rows = value.shape[0] // 2
    low, high = value[:rows], value[rows:]
    return jnp.where(bit > 0, high, low), jnp.where(bit > 0, low, high)


def as_column(row, column):
    at = (iota((8, 128), 1) == column) & (iota((8, 128), 0) == 0)
    return dot(jnp.broadcast_to(row, (8, row.shape[1])), at.astype(F32), 0, 0, lax.Precision.HIGHEST)


def hidden_back_kernel(
    spot_ref, near_ref, far_ref, hidden_ref, cot_ref, gm_ref, wo_ref, mix_ref, gwra_ref, gwrb_ref, _,
    dhid_ref, dmix_ref, keep_ref, give_ref, __,
):
    features = hidden_ref.shape[1]
    bit = spot_ref[1]
    grad = near_ref[...] + far_ref[...].astype(F32)
    unit, scale = norm_parts(hidden_ref[...])
    gain = jnp.sum(grad * unit, axis=0, keepdims=True)
    dhid = cot_ref[...].astype(F32) + norm_back(unit, scale, grad * gm_ref[...])
    dhid_ref[...] = dhid
    branch = dhid.astype(BF16)
    keep, give = halves_by(bit, dot(mix_ref[...], branch, 0, 0))
    keep_ref[:, :features], give_ref[:, :features] = keep.astype(BF16), give.astype(BF16)
    dmix_ref[...] = dot(branch, wo_ref[...], 1, 1).astype(BF16)
    experts = gwra_ref.shape[1]
    wide = (iota((experts, 128), 0) == iota((experts, 128), 1)).astype(F32)
    side = dot(gwra_ref[...] + gwrb_ref[...], wide, precision=lax.Precision.HIGHEST)
    side = side + as_column(gain, experts)
    keep, give = halves_by(bit, side)
    keep_ref[:, features:], give_ref[:, features:] = keep.astype(BF16), give.astype(BF16)


def head_pair_back(offset, dmix_ref, proj_ref, mix_ref, prob_ref, dproj_ref):
    step = pl.program_id(0)
    tokens, features = mix_ref.shape
    width = dproj_ref.shape[1] // 3
    at = lambda part: pl.ds(pl.multiple_of(part * features + (step + offset) * 128, 128), 128)
    query, keys, value = proj_ref[:, at(0)], proj_ref[:, at(1)], proj_ref[:, at(2)]
    dmix = dmix_ref[:, at(0)]
    product = dmix.astype(F32) * mix_ref[:, at(0)].astype(F32)
    first = iota((tokens, 128), 1) < HEAD_DIM
    parts = []
    for h in (0, 1):
        mine = first if h == 0 else ~first
        own_dmix = jnp.where(mine, dmix.astype(F32), 0.0).astype(BF16)
        delta = jnp.sum(jnp.where(mine, product, 0.0), axis=-1, keepdims=True)
        prob = prob_ref[h]
        dprob = dot(own_dmix, value, 1, 1)
        dscore = (prob.astype(F32) * (dprob - delta) * HEAD_DIM ** (-0.5)).astype(BF16)
        parts.append((dot(dscore, keys), dot(dscore, query, 0, 0), dot(prob, dmix, 0, 0)))
    for part in range(3):
        to = pl.ds(pl.multiple_of(part * width + step * 128, 128), 128)
        dproj_ref[:, to] = jnp.where(first, parts[0][part], parts[1][part]).astype(BF16)


def first_heads_kernel(
    spot_ref, dmix_ref, normed_ref, proj_ref, mix_ref, prob_ref, keep_ref, give_ref, dproj_ref,
):
    head_pair_back(0, dmix_ref, proj_ref, mix_ref, prob_ref, dproj_ref)

    @pl.when(pl.program_id(0) == pl.num_programs(0) - 1)
    def _():
        keep, give = halves_by(spot_ref[1], dot(normed_ref[...], dproj_ref[...], 0, 0))
        keep_ref[...], give_ref[...] = keep.astype(BF16), give.astype(BF16)


def last_heads_kernel(
    spot_ref, dmix_ref, normed_ref, proj_ref, mix_ref, prob_ref, other_ref, dhid_ref, tok_ref, ga_ref, wqkv_ref,
    gtok_ref, keep_ref, give_ref, dproj_ref,
):
    head_pair_back(pl.num_programs(0), dmix_ref, proj_ref, mix_ref, prob_ref, dproj_ref)
    tokens, features = tok_ref.shape
    width = dproj_ref.shape[1]

    @pl.when(pl.program_id(0) == pl.num_programs(0) - 1)
    def _():
        keep, give = halves_by(spot_ref[1], dot(normed_ref[...], dproj_ref[...], 0, 0))
        keep_ref[:, :width], give_ref[:, :width] = keep.astype(BF16), give.astype(BF16)
        grad = jnp.zeros((tokens, features), F32)
        half = features // 2
        for part in range(3):
            at = slice(part * half, (part + 1) * half)
            for place, ref in ((0, other_ref), (1, dproj_ref)):
                start = part * features + place * half
                grad = grad + dot(ref[:, at], wqkv_ref[:, start : start + half], 1, 1)
        unit, scale = norm_parts(tok_ref[...].astype(F32))
        gtok_ref[...] = dhid_ref[...] + norm_back(unit, scale, grad * ga_ref[...])
        side = as_column(jnp.sum(grad * unit, axis=0, keepdims=True), 0)
        keep, give = halves_by(spot_ref[1], side)
        keep_ref[:, width:], give_ref[:, width:] = keep.astype(BF16), give.astype(BF16)


def take(refs, count):
    return refs[:count], refs[count:]


def expert_kernel(pieces, group, near, *refs):
    step = pl.program_id(0)
    (spot_ref, wr_ref, own_ref, win_ref, wout_ref), refs = take(refs, 5)
    mine = (spot_ref[0] - spot_ref[3]) ^ step
    if near:
        x_refs, refs = take(refs, group)
        g_refs, refs = take(refs, group)
        back_refs, refs = take(refs, group)
    else:
        (far_ref,), refs = take(refs, 1)
        refs = refs[4:]
        dx_refs, refs = take(refs, group)
        y_refs, refs = take(refs, group)
    gwr_ref, dexp_ref, xcopy_ref, act_ref, dpre_ref, now_ref = refs
    slots = dexp_ref.shape[0]
    if near:
        for j in range(group):

            @pl.when(step == j)
            def _():
                xcopy_ref[...] = x_refs[j][...]
                now_ref[...] = g_refs[j][...]

    else:
        xcopy_ref[...] = far_ref[mine, :slots, :]
        now_ref[...] = far_ref[mine, slots:, :]

    x = xcopy_ref[...]
    g = now_ref[...].astype(F32)
    logits = dot(x, wr_ref[...])
    exponent = jnp.exp(logits - jnp.max(logits, axis=-1, keepdims=True))
    router = exponent / jnp.sum(exponent, axis=-1, keepdims=True)
    gate = jnp.sum(router * own_ref[...], axis=-1, keepdims=True)
    dexp = (gate * g).astype(BF16)
    dexp_ref[...] = dexp
    out = jnp.zeros(x.shape, F32)
    dx = jnp.zeros(x.shape, F32)
    width = win_ref.shape[1] // pieces
    for r in range(pieces):
        at = slice(r * width, (r + 1) * width)
        pre = dot(x, win_ref[:, at])
        square = pre * pre
        bend = jnp.tanh(0.7978845608028654 * pre * (1.0 + 0.044715 * square))
        half = 0.5 * (1.0 + bend)
        slope = half + (0.5 * 0.7978845608028654) * pre * (1.0 - bend * bend) * (1.0 + 0.134145 * square)
        active = (pre * half).astype(BF16)
        act_ref[:, at] = active
        dpreact = (dot(dexp, wout_ref[at, :], 1, 1) * slope).astype(BF16)
        dpre_ref[:, at] = dpreact
        out = out + dot(active, wout_ref[at, :])
        dx = dx + dot(dpreact, win_ref[:, at], 1, 1)
    out = out.astype(BF16).astype(F32)
    y = (gate * out).astype(BF16)
    dgate = jnp.sum(g * out, axis=-1, keepdims=True)
    dlogits = (dgate * gate * (own_ref[...] - router)).astype(BF16)
    dx = (dx + dot(dlogits, wr_ref[...], 1, 1)).astype(BF16)
    if near:
        for j in range(group):

            @pl.when(step == j)
            def _():
                back_refs[j][:slots, :] = dx
                back_refs[j][slots:, :] = y

    else:
        for j in range(group):

            @pl.when(step == j)
            def _():
                y_refs[j][...] = y
                dx_refs[j][...] = dx

    @pl.when(step == 0)
    def _():
        gwr_ref[...] = jnp.zeros(gwr_ref.shape, F32)

    gwr_ref[...] += dot(x, dlogits, 0, 0)


def swap(value, axis, bit):
    size = lax.axis_size(axis)
    return lax.ppermute(value, axis, [(i, i ^ bit) for i in range(size)])


def bits_of(axis):
    size = lax.axis_size(axis)
    return [1 << b for b in range(size.bit_length() - 1)]


def half_sum_kernel(at, spot_ref, keep_ref, other_ref, next_ref, give_ref):
    total = keep_ref[...].astype(F32) + other_ref[...].astype(F32)
    keep, give = halves_by(spot_ref[at], total)
    next_ref[...], give_ref[...] = keep.astype(BF16), give.astype(BF16)


def deal_kernel(groups, spot_ref, keep_ref, other_ref, own_ref, *refs):
    out_refs, total_ref = refs[:-1], refs[-1]
    total = keep_ref[...].astype(F32) + other_ref[...].astype(F32)
    rows, columns = total.shape
    total_ref[...] = total.reshape(groups, rows // groups, columns)
    own_ref[...] = total_ref[spot_ref[5]]
    for j, out_ref in enumerate(out_refs):
        out_ref[...] = total_ref[spot_ref[5] ^ (j + 1)].astype(BF16)


def pile_kernel(own_ref, *refs):
    total = own_ref[...]
    for ref in refs[:-1]:
        total = total + ref[...].astype(F32)
    refs[-1][...] = total.astype(BF16)


def line_up_kernel(spot_ref, *refs):
    out_ref, total_ref = refs[-2:]
    for j, ref in enumerate(refs[:-2]):
        total_ref[spot_ref[5] ^ j] = ref[...].astype(F32)
    out_ref[...] = total_ref[...].reshape(out_ref.shape).astype(BF16)


def finish_kernel(orders, spot_ref, *refs):
    piece_refs, out_refs = refs[: 8 * len(orders)], refs[8 * len(orders) :]
    for place, (first, second, targets) in enumerate(orders):
        for k in range(8):
            ref = piece_refs[8 * place + k]
            rows = ref.shape[0]
            spot = (
                (spot_ref[1] ^ (k >> 2)) * 4 + (spot_ref[first] ^ (k >> 1 & 1)) * 2 + (spot_ref[second] ^ (k & 1))
            )
            at = pl.ds(pl.multiple_of(spot * rows, 8), rows)
            for start, width, out, column in targets:
                out_refs[out][at, column : column + width] = ref[:, start : start + width].astype(F32)


LINKS = {2: ("dp", 2), 4: ("expert", 1)}


def halve(spot, at, keep, arrived, *after):
    scalar = pl.BlockSpec(memory_space=pltpu.SMEM)
    part = (keep.shape[0] // 2, keep.shape[1])
    keep, give = call(
        functools.partial(half_sum_kernel, at), (1,), (spot, keep, arrived),
        [scalar, whole(keep.shape), whole(keep.shape)],
        [shape_of(part, BF16)] * 2, [whole_out(part)] * 2,
        after=after,
    )
    return keep, swap(give, *LINKS[at])


def deal_out(spot, keep, arrived, groups):
    scalar = pl.BlockSpec(memory_space=pltpu.SMEM)
    rows, columns = keep.shape
    piece = (rows // groups, columns)
    dealt = call(
        functools.partial(deal_kernel, groups), (1,), (spot, keep, arrived),
        [scalar, whole(keep.shape), whole(keep.shape)],
        (shape_of(piece, F32), *[shape_of(piece, BF16)] * (groups - 1)),
        (whole_out(piece),) * groups,
        [pltpu.VMEM((groups, *piece), F32)],
    )
    total = call(
        pile_kernel, (1,), (dealt[0], *[swap(v, "expert", 2 * (j + 1)) for j, v in enumerate(dealt[1:])]),
        [whole(piece)] * groups, shape_of(piece, BF16), whole_out(piece),
    )
    own = call(
        line_up_kernel, (1,), (spot, total, *[swap(total, "expert", 2 * j) for j in range(1, groups)]),
        [scalar] + [whole(piece)] * groups,
        shape_of(keep.shape, BF16), whole_out(keep.shape), [pltpu.VMEM((groups, *piece), F32)],
    )
    pieces = [own]
    for link in (LINKS[4], LINKS[2], ("dp", 1)):
        pieces = pieces + [swap(v, *link) for v in pieces]
    return pieces


def all_sum(value, steps):
    rows = value.shape[0]
    place = []
    for axis, bit in steps:
        half = value.shape[0] // 2
        mine = ((lax.axis_index(axis) & bit) > 0).astype(jnp.int32)
        keep = lax.dynamic_slice_in_dim(value, mine * half, half, 0)
        give = lax.dynamic_slice_in_dim(value, (1 - mine) * half, half, 0)
        value = (keep.astype(F32) + swap(give, axis, bit).astype(F32)).astype(BF16)
        place.append(mine)
    for (axis, bit), mine in zip(reversed(steps), reversed(place)):
        other = swap(value, axis, bit)
        low = jnp.where(mine > 0, other, value)
        high = jnp.where(mine > 0, value, other)
        value = jnp.concatenate([low, high], axis=0)
    return value


def local(
    tokens, segment_ids, pad_mask, routes, priority, gain_attn, w_qkv, w_o, gain_moe, w_router,
    w_in, w_out, cotangent,
):
    sequences, length, features = tokens.shape
    count = sequences * length
    experts = w_router.shape[1]
    groups = lax.axis_size("expert")
    replicas = lax.axis_size("dp")
    devices = groups * replicas
    group = groups // 2
    most = 4 * count // experts
    slots = -(-most // 16) * 16
    capacity = (42 * count * devices + 20 * experts - 1) // (20 * experts)
    me = lax.axis_index(("dp", "expert")).astype(jnp.int32).reshape(1)
    replica = lax.axis_index("dp")
    column = lax.axis_index("expert")
    spot = jnp.stack(
        [column, replica & 1, replica >> 1 & 1, column // group * group, column & 1, column >> 1]
    ).astype(jnp.int32)
    tok = tokens.reshape(count, features)
    cot = cotangent.reshape(count, features)
    ga = gain_attn.reshape(1, features)
    gm = gain_moe.reshape(1, features)
    full = (count, features)
    scalar = pl.BlockSpec(memory_space=pltpu.SMEM)
    sent = shape_of((slots, features), BF16)

    def across(value):
        return swap(value, "expert", group)

    def among(values):
        return [v if j == 0 else swap(v, "expert", j) for j, v in enumerate(values)]

    def spread(target, rows, us, *after):
        return call(
            functools.partial(spread_kernel, slots),
            (1,),
            (spot, target, rows),
            [scalar, whole((8, count)), whole(full)],
            [sent] * group,
            [whole_out((slots, features))] * group,
            us=us,
            after=after,
        )

    halves = [list(range(group)), list(range(group, groups))]
    joint = (group, 2 * slots, features)

    def half_exchange(value):
        return lax.all_to_all(value, "expert", 0, 0, axis_index_groups=halves, tiled=True)

    far_cot = across(cot)
    full_in = lax.all_gather(w_in[0], "dp", axis=1, tiled=True)
    full_out = lax.all_gather(w_out[0], "dp", axis=0, tiled=True)

    hist, info, target = call(
        functools.partial(route_kernel, slots, experts),
        (1,),
        (routes.reshape(count, 2), priority.reshape(1, count), pad_mask.reshape(1, count)),
        [whole((count, 2)), whole((1, count)), whole((1, count))],
        (shape_of((experts, BINS), jnp.int32), shape_of((8, count), F32), shape_of((8, count), jnp.int32)),
        (whole_out((experts, BINS)), whole_out((8, count)), whole_out((8, count))),
    )
    far_target = across(target)
    near_g_sent = spread(target, cot, 1)
    near_g = among(near_g_sent)
    every = lax.all_to_all(
        jnp.broadcast_to(hist[None], (devices, experts, BINS)), ("dp", "expert"), 0, 0, tiled=True
    )

    pairs = features // 128
    tile = lambda dtype: shape_of((count, features), dtype)
    prob_block = pl.BlockSpec((2, count, count), lambda i: (i, 0, 0))
    normed, proj, mix, prob = call(
        attend_kernel,
        (pairs,),
        (tok, segment_ids.reshape(1, count), pad_mask.reshape(1, count), ga, w_qkv),
        [whole(full), whole((1, count)), whole((1, count)), whole((1, features)), whole(w_qkv.shape)],
        (tile(BF16), shape_of((count, 3 * features), BF16), tile(BF16), shape_of((HEADS, count, count), BF16)),
        (whole_out(full), whole_out((count, 3 * features)), whole_out(full), prob_block),
        [pltpu.VMEM((count, count), F32)],
        us=20000,
        after=(near_g_sent[0],),
    )
    kept, hidden, normed_moe = call(
        functools.partial(keep_kernel, capacity),
        (1,),
        (me, every, info, target, tok, mix, w_o, gm),
        [scalar, whole((devices, experts, BINS)), whole((8, count)), whole((8, count)), whole(full), whole(full), whole(w_o.shape), whole((1, features))],
        (shape_of((8, count), jnp.int32), tile(F32), tile(BF16)),
        (whole_out((8, count)), whole_out(full), whole_out(full)),
    )
    far_x = across(normed_moe)
    far_kept = across(kept)
    near_x = spread(kept, normed_moe, 20000, *near_g)
    near_x_sent, near_x = near_x, among(near_x)
    far_sent = call(
        functools.partial(spread_joint_kernel, slots),
        (group,),
        (spot, far_kept, far_target, far_x, far_cot),
        [scalar] + [whole((8, count))] * 2 + [whole(full)] * 2,
        shape_of(joint, BF16),
        pl.BlockSpec((1, 2 * slots, features), lambda e: (e, 0, 0)),
        after=(near_x_sent[0], *near_x[1:]),
    )
    far_rows = half_exchange(far_sent)

    hidden_units = w_out.shape[1] * replicas
    own = (iota((1, experts), 1) == column).astype(F32)
    flat = group * slots
    slot_spec = whole_out((slots, features))
    weights = (spot, w_router, own, full_in, full_out)
    weight_specs = [scalar, whole(w_router.shape), whole((1, experts)), whole(full_in.shape), whole(full_out.shape)]
    tall = [shape_of((2 * flat, n), BF16) for n in (features, features, hidden_units, hidden_units)]
    tall_blocks = lambda first: [
        pl.BlockSpec((slots, v.shape[1]), lambda e: (first + e, 0)) for v in tall
    ]
    outs = call(
        functools.partial(expert_kernel, 4, group, True),
        (group,),
        (*weights, *near_x, *near_g),
        weight_specs + [whole((slots, features))] * (2 * group),
        (*[shape_of((2 * slots, features), BF16)] * group, shape_of(w_router.shape, F32), *tall),
        (*[whole_out((2 * slots, features))] * group, whole_out(w_router.shape), *tall_blocks(0)),
        [pltpu.VMEM((slots, features), BF16)],
        us=35000,
        after=(far_sent,),
    )
    near_back, outs = take(outs, group)
    near_back = among(near_back)
    gwr_a, kept_rows = outs[0], outs[1:]
    outs = call(
        functools.partial(expert_kernel, 4, group, False),
        (group,),
        (*weights, far_rows, *kept_rows),
        weight_specs + [whole(joint)] + [pl.BlockSpec(memory_space=pl.ANY)] * 4,
        (*[sent] * (2 * group), shape_of(w_router.shape, F32), *tall),
        (*[slot_spec] * (2 * group), whole_out(w_router.shape), *tall_blocks(group)),
        [pltpu.VMEM((slots, features), BF16)],
        after=(gwr_a,),
        alias=[(6 + i, 2 * group + 1 + i) for i in range(4)],
    )
    d_far, outs = take(outs, group)
    y_far, outs = take(outs, group)
    gwr_b, all_dexp, all_x, all_act, all_dpre = outs
    d_far, y_far = among(d_far), among(y_far)
    near_d, block_part = call(
        near_kernel,
        (1,),
        (spot, kept, hidden, *near_back),
        [scalar, whole((8, count)), whole(full)] + [whole((2 * slots, features))] * group,
        (tile(F32), tile(F32)),
        (whole_out(full), whole_out(full)),
        after=(gwr_b,),
    )

    def gather(rows, *after):
        return call(
            gather_kernel,
            (1,),
            (spot, far_kept, *rows),
            [scalar, whole((8, count))] + [whole((slots, features))] * group,
            tile(BF16),
            whole_out(full),
            after=after,
        )

    anywhere = pl.BlockSpec(memory_space=pl.ANY)
    part = hidden_units // 4
    gout = call(
        left_grad_kernel,
        (4,),
        (all_act, all_dexp),
        [pl.BlockSpec((2 * flat, part), lambda i: (0, i)), whole((2 * flat, features))],
        shape_of((hidden_units, features), BF16),
        pl.BlockSpec((part, features), lambda i: (i, 0)),
        after=(near_d,),
    )
    d_far = gather(d_far, gout)
    gin, gout = call(
        right_grad_kernel,
        (4,),
        (all_x, all_dpre, gout),
        [whole((2 * flat, features)), pl.BlockSpec((2 * flat, part), lambda i: (0, i)), anywhere],
        (shape_of((features, hidden_units), BF16), shape_of((hidden_units, features), BF16)),
        (pl.BlockSpec((features, part), lambda i: (0, i)), anywhere),
        after=(d_far,),
        alias=[(2, 1)],
    )
    y_far = gather(y_far, gin)
    d_far = across(d_far)
    gout = lax.psum_scatter(gout, "dp", scatter_dimension=0, tiled=True).astype(F32)
    gin = lax.psum_scatter(gin, "dp", scatter_dimension=1, tiled=True).astype(F32)

    o_half = (features // 2, features + 128)
    a_half = (features // 2, 3 * features // 2)
    b_half = (features // 2, 3 * features // 2 + 128)
    dhid, dmix, keep_o, give_o, y_far = call(
        hidden_back_kernel,
        (1,),
        (spot, near_d, d_far, hidden, cot, gm, w_o, mix, gwr_a, gwr_b, y_far),
        [scalar] + [whole(full)] * 4 + [whole((1, features)), whole(w_o.shape), whole(full)] + [whole(gwr_a.shape)] * 2 + [anywhere],
        (tile(F32), tile(BF16), *[shape_of(o_half, BF16)] * 2, tile(BF16)),
        (whole_out(full), whole_out(full), *[whole_out(o_half)] * 2, anywhere),
        alias=[(10, 4)],
    )
    y_far = across(y_far)
    some = 3 * features // 2
    head_specs = lambda offset: [scalar] + [whole(full)] * 2 + [whole((count, 3 * features)), whole(full)] + [
        pl.BlockSpec((2, count, count), lambda i: (i + offset, 0, 0))
    ]
    keep_a, give_a, dproj_a = call(
        first_heads_kernel,
        (pairs // 2,),
        (spot, dmix, normed, proj, mix, prob),
        head_specs(0),
        (shape_of(a_half, BF16), shape_of(a_half, BF16), shape_of((count, some), BF16)),
        (whole_out(a_half), whole_out(a_half), whole_out((count, some))),
        us=13000,
    )
    by_hand = replicas == 4 and groups == 8 and features % (8 * devices) == 0
    if by_hand:
        sum_o = halve(spot, 2, keep_o, swap(give_o, "dp", 1), dproj_a)
    gtok, keep_b, give_b = call(
        last_heads_kernel,
        (pairs // 2,),
        (spot, dmix, normed, proj, mix, prob, dproj_a, dhid, tok, ga, w_qkv),
        head_specs(pairs // 2) + [whole((count, some)), whole(full), whole(full), whole((1, features)), whole(w_qkv.shape)],
        (tile(F32), shape_of(b_half, BF16), shape_of(b_half, BF16)),
        (whole_out(full), whole_out(b_half), whole_out(b_half)),
        [pltpu.VMEM((count, some), BF16)],
        us=14000,
        after=sum_o[:1] if by_hand else (),
    )
    block_out = call(
        block_kernel,
        (1,),
        (block_part, y_far),
        [whole(full)] * 2,
        tile(BF16),
        whole_out(full),
        after=(gtok,),
    )
    if by_hand:
        rows = groups // 2
        sum_a = halve(spot, 2, keep_a, swap(give_a, "dp", 1), gtok)
        sum_o = halve(spot, 4, *sum_o)
        sum_b = halve(spot, 2, keep_b, swap(give_b, "dp", 1), sum_o[0], sum_a[0])
        sum_a = halve(spot, 4, *sum_a)
        sum_b = halve(spot, 4, *sum_b)
        pieces = [v for total in (sum_o, sum_a, sum_b) for v in deal_out(spot, *total, rows)]
        half = features // 2
        heads = lambda place: tuple(
            (part * half, half, 2, part * features + place * half) for part in range(3)
        )
        orders = (
            (2, 4, ((0, features, 0, 0), (features, 128, 1, 0))),
            (2, 4, heads(0)),
            (2, 4, heads(1) + ((some, 128, 3, 0),)),
        )
        shapes = [(features, features), (features, 128), (features, 3 * features), (features, 128)]
        grad_o, side_o, grad_qkv, side_q = call(
            functools.partial(finish_kernel, orders),
            (1,),
            (spot, *pieces),
            [scalar] + [whole(v.shape) for v in pieces],
            [shape_of(v, F32) for v in shapes],
            [whole_out(v) for v in shapes],
            after=(gin, gout),
        )
    else:
        low = (replica & 1) == 0

        def rejoin(keep, give):
            return jnp.concatenate([jnp.where(low, keep, give), jnp.where(low, give, keep)], axis=0)

        gain_steps = [("dp", b) for b in bits_of("dp")] + [("expert", b) for b in bits_of("expert")]
        both = all_sum(rejoin(keep_o, give_o), gain_steps).astype(F32)
        grad_o, side_o = both[:, :features], both[:, features:]
        first = all_sum(rejoin(keep_a, give_a), gain_steps).astype(F32)
        last = all_sum(rejoin(keep_b, give_b), gain_steps).astype(F32)
        half = features // 2
        cut = lambda part: slice(part * half, (part + 1) * half)
        grad_qkv = jnp.concatenate([v[:, cut(part)] for part in range(3) for v in (first, last)], axis=1)
        side_q = last[:, some:]
    return (
        block_out.reshape(sequences, length, features),
        gtok.reshape(sequences, length, features),
        side_q[:, 0],
        grad_qkv,
        grad_o,
        side_o[:, experts],
        side_o[:, :experts],
        gin[None],
        gout[None],
    )


def solution(mesh):
    rows = P(("dp", "expert"), None, None)
    flat = P(("dp", "expert"), None)
    first = P("expert", None, "dp")
    second = P("expert", "dp", None)
    return jax.shard_map(
        local,
        mesh=mesh,
        in_specs=(rows, flat, flat, rows, flat, P(), P(), P(), P(), P(), first, second, rows),
        out_specs=(rows, rows, P(), P(), P(), P(), P(), first, second),
        check_vma=False,
    )
```

time: 659 us -> 531 us (0.81)
  waiting for transfers between devices: 385 us -> 143 us
  Pallas kernels: 150 us -> 240 us
  starting transfers between devices: 42.5 us -> 89 us
  matrix products: 27.5 us -> 0 us
  other arithmetic: 24.6 us -> 8.23 us
  between operations: 1.52 us -> 14.8 us
    all_to_all x4 -> x1, waiting for transfers between devices: 149 us -> 0.01 us  [half_exchange(): lax.all_to_all(value, 'expert', 0, 0, axis_index_groups=halves, tiled=True)]
    ppermute x22 -> x69, waiting for transfers between devices: 235 us -> 141 us  [swap(): return lax.ppermute(value, axis, [(i, i ^ bit) for i in range(size)])]
    pallas_call x7 -> x33, Pallas kernels: 150 us -> 240 us  [call(): pl.pallas_call(body, grid=grid, in_specs=[pl.BlockSpec(memory_space=pl.AN...]
    ppermute x22 -> x69, starting transfers between devices: 17.4 us -> 80.9 us  [swap(): return lax.ppermute(value, axis, [(i, i ^ bit) for i in range(size)])]
    dot_general x8 -> x0, matrix products: 27.5 us -> none  [dot(): lax.dot_general(a, b, (((ca,), (cb,)), ((), ())), precision=precision, pr...]
    all_to_all x4 -> x1, starting transfers between devices: 17.8 us -> 3.87 us  [half_exchange(): lax.all_to_all(value, 'expert', 0, 0, axis_index_groups=halves, tiled=True)]
    unnamed x41 -> x159, local copies, waits for them, and re-layouts: 13.5 us -> 21 us
  transfers between devices with their start and end apart: 27 -> 75, of which waited for: 18 -> 23; matrix products, arithmetic and copies ran while one was open for 6% -> 3% of each run, Pallas kernels for 7% -> 41%
where the time goes in v2:
time: 531 us; the launch traced here: 521 us
  Pallas kernels  240 us (45%)
  waiting for transfers between devices  143 us (27%)
  starting transfers between devices  89 us (17%)
  local copies, waits for them, and re-layouts  26.3 us (5%)
  between operations  14.8 us (3%)
  other arithmetic  8.23 us (2%)
    pallas_call x33, Pallas kernels, call(): pl.pallas_call(body, grid=grid, in_specs=[pl.BlockSpec(memory_space=pl.AN...  240 us
    ppermute x69, waiting for transfers between devices, swap(): return lax.ppermute(value, axis, [(i, i ^ bit) for i in range(size)])  141 us
    ppermute x69, starting transfers between devices, swap(): return lax.ppermute(value, axis, [(i, i ^ bit) for i in range(size)])  80.9 us
    unnamed x159, local copies, waits for them, and re-layouts  21 us
  transfers between devices with their start and end apart: 75, of which 23 were waited for; matrix products, arithmetic and copies ran while one was open for 3% of the time, Pallas kernels for 41%

profile of v2, /device:TPU:0, one launch (start us, length us, event | category | flops | bytes accessed | tf_op | source)
XLA Modules:
  0.0 521.1 jit_solution(207879535782656280)
XLA Ops:
  12.0 4.0 collective-permute-start.7
  17.4 3.8 all-to-all-start
  32.2 18.2 %shard_map.198 = (bf16[576,768]{1,0:T(8,128)(2,1)}, bf16[576,2304]{1,0:T(8,128)(2,1)}, bf16[576,768]{1,0:T(8,128)(2,1)}, bf16[12,576,576]{2,1,0:T(8,128)(2,1)}) custom-call(bf16[288,768]{1,0:T(8,128)(2,1)} %get-tuple-element.93.refs_0_.refs_10_, bf16[576,768]{1,0:T(8,128)(2,1)} %bitcast.29, s32[1,576]{1,0:T(1,128)} %refs_2_.5, s32[1,576]{1,0:T(1,128)} %refs_3_.1, ...), custom_call_target="tpu_custom_call" | custom-call | flops 20000000000 | tf_op jit(solution)/shard_map/pallas_call | solution.py:45
  51.6 5.2 shard_map.199
  60.5 9.4 %collective-permute-done.2.refs_3_.refs_13_ = bf16[288,768]{1,0:T(8,128)(2,1)} collective-permute-done((bf16[288,768]{1,0:T(8,128)(2,1)}, bf16[288,768]{1,0:T(8,128)(2,1)}, u32[]{:S(2)}, u32[]{:S(2)}) %collective-permute-start.2) | collective-permute-done | bytes 442400 | tf_op jit(solution)/shard_map/ppermute | solution.py:418
  75.6 10.6 %collective-permute-done.6.refs_5_.refs_2_ = s32[8,576]{1,0:T(8,128)S(1)} collective-permute-done((s32[8,576]{1,0:T(8,128)}, s32[8,576]{1,0:T(8,128)S(1)}, u32[]{:S(2)}, u32[]{:S(2)}) %collective-permute-start.6) | collective-permute-done | bytes 18464 | tf_op jit(solution)/shard_map/ppermute | solution.py:418
  86.2 20.4 %collective-permute-done.4.refs_2_.refs_8_ = bf16[288,768]{1,0:T(8,128)(2,1)S(1)} collective-permute-done((bf16[288,768]{1,0:T(8,128)(2,1)}, bf16[288,768]{1,0:T(8,128)(2,1)S(1)}, u32[]{:S(2)}, u32[]{:S(2)}) %collective-permute-start.4) | collective-permute-done | bytes 442400 | tf_op jit(solution)/shard_map/ppermute | solution.py:418
  106.6 8.2 %collective-permute-done.5.refs_3_.refs_9_ = bf16[288,768]{1,0:T(8,128)(2,1)S(1)} collective-permute-done((bf16[288,768]{1,0:T(8,128)(2,1)}, bf16[288,768]{1,0:T(8,128)(2,1)S(1)}, u32[]{:S(2)}, u32[]{:S(2)}) %collective-permute-start.5) | collective-permute-done | bytes 442400 | tf_op jit(solution)/shard_map/ppermute | solution.py:418
  115.9 5.9 %shard_map.201.refs_0_ = bf16[4,576,768]{2,1,0:T(8,128)(2,1)} custom-call(bf16[288,768]{1,0:T(8,128)(2,1)} %get-tuple-element.102.refs_0_.refs_6_, bf16[288,768]{1,0:T(8,128)(2,1)} %copy-done.14, bf16[288,768]{1,0:T(8,128)(2,1)} %copy-done.15, bf16[288,768]{1,0:T(8,128)(2,1)} %copy-done.16, s32[6]{0:T(128)} %stack.27.refs_0_.refs_4_.refs_1_.refs_2_, ...), custom_call_target="tpu_custom_call" | custom-call | flops 1000000 | tf_op jit(solution)/shard_map/pallas_call | solution.py:45
  121.8 3.9 all-to-all-start.1
  127.4 37.0 %shard_map.202 = (bf16[576,768]{1,0:T(8,128)(2,1)}, bf16[576,768]{1,0:T(8,128)(2,1)}, bf16[576,768]{1,0:T(8,128)(2,1)}, bf16[576,768]{1,0:T(8,128)(2,1)}, f32[76...) custom-call(bf16[4,576,768]{2,1,0:T(8,128)(2,1)} %shard_map.201.refs, ...), custom_call_target="tpu_custom_call" | custom-call | flops 35000000512 | tf_op jit(solution)/shard_map/pallas_call | solution.py:45
  169.7 37.1 %shard_map.203 = (bf16[288,768]{1,0:T(8,128)(2,1)}, bf16[288,768]{1,0:T(8,128)(2,1)}, bf16[288,768]{1,0:T(8,128)(2,1)}, bf16[288,768]{1,0:T(8,128)(2,1)}, bf16[2...) custom-call(f32[768,8]{1,0:T(8,128)} %get-tuple-element.106.refs_0_., ...), custom_call_target="tpu_custom_call", output_to_operand_aliasing={{9}: (7, {}), {10}: (8, {}), {11}: (9, {}), {12}: (10, {})} | custom-call | flops 1000000 | tf_op jit(solution)/shard_map/pallas_call | solution.py:45
  210.4 7.9 %shard_map.204 = (f32[576,768]{1,0:T(8,128)}, f32[576,768]{1,0:T(8,128)}) custom-call(f32[768,8]{1,0:T(8,128)} %get-tuple-element.111.refs_0_.refs_9_, s32[6]{0:T(128)} %stack.27.refs_0_.refs_4_.refs_1_.refs_2_, s32[8,576]{1,0:T(8,128)} %get-tuple-element.100.refs_5_.refs_2_, f32[576,768]{1,0:T(8,128)} %get-tuple-element.112.refs_3_, ...), custom_call_target="tpu_custom_call" | custom-call | flops 1000000 | tf_op jit(solution)/shard_map/pallas_call | solution.py:45
  218.3 16.1 %shard_map.205.refs_0_.refs_3_ = bf16[3072,768]{1,0:T(8,128)(2,1)} custom-call(f32[576,768]{1,0:T(8,128)} %get-tuple-element.117.refs_0_.refs_1_, bf16[2304,3072]{1,0:T(8,128)(2,1)} %get-tuple-element.118.refs_1_, bf16[2304,768]{1,0:T(8,128)(2,1)} %get-tuple-element.119.refs_2_), custom_call_target="tpu_custom_call" | custom-call | flops 1000000 | tf_op jit(solution)/shard_map/pallas_call | solution.py:45
  235.5 4.4 shard_map.206.refs_0_
  239.9 16.0 %shard_map.207 = (bf16[768,3072]{1,0:T(8,128)(2,1)}, bf16[3072,768]{1,0:T(8,128)(2,1)}) custom-call(bf16[576,768]{1,0:T(8,128)(2,1)} %shard_map.206.refs_0_, bf16[2304,768]{1,0:T(8,128)(2,1)} %get-tuple-element.124.refs_1_, bf16[2304,3072]{1,0:T(8,128)(2,1)} %get-tuple-element.125.refs_2_, ...), custom_call_target="tpu_custom_call", output_to_operand_aliasing={{1}: (3, {})} | custom-call | flops 1000000 | tf_op jit(solution)/shard_map/pallas_call | solution.py:45
  261.9 7.2 %collective-permute-done.17.refs_4_ = bf16[288,768]{1,0:T(8,128)(2,1)S(1)} collective-permute-done((bf16[288,768]{1,0:T(8,128)(2,1)}, bf16[288,768]{1,0:T(8,128)(2,1)S(1)}, u32[]{:S(2)}, u32[]{:S(2)}) %collective-permute-start.17) | collective-permute-done | bytes 442400 | tf_op jit(solution)/shard_map/ppermute | solution.py:418
  269.1 18.9 %collective-permute-done.18.refs_5_ = bf16[288,768]{1,0:T(8,128)(2,1)S(1)} collective-permute-done((bf16[288,768]{1,0:T(8,128)(2,1)S(1)}, bf16[288,768]{1,0:T(8,128)(2,1)S(1)}, u32[]{:S(2)}, u32[]{:S(2)}) %collective-permute-start.18) | collective-permute-done | bytes 442400 | tf_op jit(solution)/shard_map/ppermute | solution.py:418
  288.0 6.2 %collective-permute-done.19.refs_6_ = bf16[288,768]{1,0:T(8,128)(2,1)S(1)} collective-permute-done((bf16[288,768]{1,0:T(8,128)(2,1)S(1)}, bf16[288,768]{1,0:T(8,128)(2,1)S(1)}, u32[]{:S(2)}, u32[]{:S(2)}) %collective-permute-start.19) | collective-permute-done | bytes 442400 | tf_op jit(solution)/shard_map/ppermute | solution.py:418
  295.0 4.4 shard_map.208.refs_10_
  300.4 8.1 %shard_map.209 = (f32[576,768]{1,0:T(8,128)}, bf16[576,768]{1,0:T(8,128)(2,1)}, bf16[384,896]{1,0:T(8,128)(2,1)}, bf16[384,896]{1,0:T(8,128)(2,1)}, bf16[576,768]{1,0:T(8,128)(2,1)}) custom-call(s32[6]{0:T(128)} %stack.27.refs_0_.refs_4_.refs_1_.refs_2_, f32[576,768]{1,0:T(8,128)} %get-tuple-element.117.refs_0_.refs_1_, ...), custom_call_target="tpu_custom_call", output_to_operand_aliasing={{4}: (10, {})} | custom-call | flops 1000000 | tf_op jit(solution)/shard_map/pallas_call | solution.py:45
  308.4 12.2 %shard_map.210 = (bf16[384,1152]{1,0:T(8,128)(2,1)}, bf16[384,1152]{1,0:T(8,128)(2,1)}, bf16[576,1152]{1,0:T(8,128)(2,1)}) custom-call(s32[6]{0:T(128)} %stack.27.refs_0_.refs_4_.refs_1_.refs_2_, bf16[576,768]{1,0:T(8,128)(2,1)} %get-tuple-element.131.refs_1_.refs_2_, bf16[576,768]{1,0:T(8,128)(2,1)} %get-tuple-element.132.refs_2_.refs_3_, ...), custom_call_target="tpu_custom_call" | custom-call | flops 12999999488 | tf_op jit(solution)/shard_map/pallas_call | solution.py:45
  323.8 19.7 %shard_map.212 = (f32[576,768]{1,0:T(8,128)}, bf16[384,1280]{1,0:T(8,128)(2,1)}, bf16[384,1280]{1,0:T(8,128)(2,1)}) custom-call(bf16[192,896]{1,0:T(8,128)(2,1)} %get-tuple-element.138.refs_0_.refs_1_, s32[6]{0:T(128)} %stack.27.refs_0_.refs_4_.refs_1_.refs_2_, bf16[576,768]{1,0:T(8,128)(2,1)} %get-tuple-element.131.refs_1_.refs_2_, ...), custom_call_target="tpu_custom_call" | custom-call | flops 14000000000 | tf_op jit(solution)/shard_map/pallas_call | solution.py:45
  351.1 10.5 %collective-permute-done.22.refs_2_ = bf16[192,896]{1,0:T(8,128)(2,1)S(1)} collective-permute-done((bf16[192,896]{1,0:T(8,128)(2,1)S(1)}, bf16[192,896]{1,0:T(8,128)(2,1)S(1)}, u32[]{:S(2)}, u32[]{:S(2)}) %collective-permute-start.22) | collective-permute-done | bytes 344096 | tf_op jit(solution)/shard_map/ppermute | solution.py:418
  373.8 16.9 %collective-permute-done.38.refs_2_ = bf16[192,1152]{1,0:T(8,128)(2,1)S(1)} collective-permute-done((bf16[192,1152]{1,0:T(8,128)(2,1)S(1)}, bf16[192,1152]{1,0:T(8,128)(2,1)S(1)}, u32[]{:S(2)}, u32[]{:S(2)}) %collective-permute-start.38) | collective-permute-done | bytes 442400 | tf_op jit(solution)/shard_map/ppermute | solution.py:418
  438.3 5.5 %collective-permute-done.42.refs_3_ = bf16[24,1152]{1,0:T(8,128)(2,1)S(1)} collective-permute-done((bf16[24,1152]{1,0:T(8,128)(2,1)}, bf16[24,1152]{1,0:T(8,128)(2,1)S(1)}, u32[]{:S(2)}, u32[]{:S(2)}) %collective-permute-start.42) | collective-permute-done | bytes 55328 | tf_op jit(solution)/shard_map/ppermute | solution.py:418
  446.8 4.3 collective-permute-done.57.refs_2_
  483.9 3.8 convert_bitcast_fusion.1
  488.8 4.6 collective-permute-done.63.refs_21_
  493.4 4.8 collective-permute-done.64.refs_22_
  498.2 3.9 convert_bitcast_fusion
  503.1 7.2 %shard_map.228 = (f32[768,768]{1,0:T(8,128)}, f32[768,128]{1,0:T(8,128)}, f32[768,2304]{1,0:T(8,128)}, f32[768,128]{1,0:T(8,128)}) custom-call(f32[768,768]{1,0:T(8,128)} %get-tuple-element.196.refs_0_, f32[768,768]{1,0:T(8,128)} %get-tuple-element.194.refs_1_, s32[6]{0:T(128)} %stack.27.refs_0_.refs_4_.refs_1_.refs_2_, bf16[96,896]{1,0:T(8,128)(2,1)} %shard_map.217.refs_3_, ...), custom_call_target="tpu_custom_call" | custom-call | flops 1000000 | tf_op jit(solution)/shard_map/pallas_call | solution.py:45
  (322 shorter events, 160.1 us)
Async XLA Ops:
  7.2 120.2 %all-gather.5.cloned.1.call-start = ((), (), s32[]{:S(2)}) async-start(), calls=%async_computation.6 | async-start | bytes 5898240 | tf_op jit(solution)/shard_map/all_gather | solution.py:582
  7.9 119.4 %all-gather.7.cloned.1.call-start = ((), (), s32[]{:S(2)}) async-start(), calls=%async_computation.7 | async-start | bytes 5898240 | tf_op jit(solution)/shard_map/all_gather | solution.py:583
  12.0 63.0 %collective-permute-start.7 = (s32[8,576]{1,0:T(8,128)}, s32[8,576]{1,0:T(8,128)S(1)}, u32[]{:S(2)}, u32[]{:S(2)}) collective-permute-start(s32[8,576]{1,0:T(8,128)} %get-tuple-element.92.refs_1_.refs_3_), channel_id=1, source_target_pairs={{0,4},{1,5},{2,6},{3,7},{4,0},{5,1},{6,2},{7,3},{8,12},{9,13},{10,... | collective-permute-start | bytes 55304 | tf_op jit(solution)/shard_map/ppermute | solution.py:418
  17.4 33.5 %all-to-all-start = ((s32[32,8,128]{2,1,0:T(8,128)}), s32[32,8,128]{2,1,0:T(8,128)S(1)}, u32[]{:S(2)}, u32[]{:S(2)}) async-start(s32[32,8,128]{2,1,0:T(8,128)} %broadcast_in_dim.12), calls=%async_computation | async-start | bytes 262144 | tf_op jit(solution)/shard_map/all_to_all | solution.py:596
  21.2 65.0 %collective-permute-start.9 = (bf16[576,768]{1,0:T(8,128)(2,1)S(1)}, bf16[576,768]{1,0:T(8,128)(2,1)S(1)}, u32[]{:S(2)}, u32[]{:S(2)}) collective-permute-start(bf16[576,768]{1,0:T(8,128)(2,1)S(1)} %bitcast.26), channel_id=1, source_target_pairs={{0,4},{1,5},{2,6},{3,7},{4,0},{5,1},{6,2},{7,3},{8,12},{9,13},{10,... | collective-permute-start | bytes 2654216 | tf_op jit(solution)/shard_map/ppermute | solution.py:418
  28.1 28.7 %collective-permute-start = (bf16[288,768]{1,0:T(8,128)(2,1)}, bf16[288,768]{1,0:T(8,128)(2,1)S(1)}, u32[]{:S(2)}, u32[]{:S(2)}) collective-permute-start(bf16[288,768]{1,0:T(8,128)(2,1)} %get-tuple-element.94), channel_id=1, source_target_pairs={{0,1},{1,0},{2,3},{3,2},{4,5},{5,4},{6,7},{7,6},{8,9},{9,8},{10,11... | collective-permute-start | bytes 1327112 | tf_op jit(solution)/shard_map/ppermute | solution.py:418
  29.5 27.7 %collective-permute-start.1 = (bf16[288,768]{1,0:T(8,128)(2,1)}, bf16[288,768]{1,0:T(8,128)(2,1)S(1)}, u32[]{:S(2)}, u32[]{:S(2)}) collective-permute-start(bf16[288,768]{1,0:T(8,128)(2,1)} %get-tuple-element.95), channel_id=1, source_target_pairs={{0,2},{1,3},{2,0},{3,1},{4,6},{5,7},{6,4},{7,5},{8,10},{9,11},{10,... | collective-permute-start | bytes 1327112 | tf_op jit(solution)/shard_map/ppermute | solution.py:418
  31.1 38.9 %collective-permute-start.2 = (bf16[288,768]{1,0:T(8,128)(2,1)}, bf16[288,768]{1,0:T(8,128)(2,1)}, u32[]{:S(2)}, u32[]{:S(2)}) collective-permute-start(bf16[288,768]{1,0:T(8,128)(2,1)} %get-tuple-element.96), channel_id=1, source_target_pairs={{0,3},{1,2},{2,1},{3,0},{4,7},{5,6},{6,5},{7,4},{8,11},{9,10},{10,... | collective-permute-start | bytes 1327112 | tf_op jit(solution)/shard_map/ppermute | solution.py:418
  56.8 29.4 %collective-permute-start.6 = (s32[8,576]{1,0:T(8,128)}, s32[8,576]{1,0:T(8,128)S(1)}, u32[]{:S(2)}, u32[]{:S(2)}) collective-permute-start(s32[8,576]{1,0:T(8,128)} %get-tuple-element.100.refs_5_.refs_2_), channel_id=1, source_target_pairs={{0,4},{1,5},{2,6},{3,7},{4,0},{5,1},{6,2},{7,3},{8,12},{9,13},{10,... | collective-permute-start | bytes 55304 | tf_op jit(solution)/shard_map/ppermute | solution.py:418
  58.0 56.8 %collective-permute-start.8 = (bf16[576,768]{1,0:T(8,128)(2,1)}, bf16[576,768]{1,0:T(8,128)(2,1)S(1)}, u32[]{:S(2)}, u32[]{:S(2)}) collective-permute-start(bf16[576,768]{1,0:T(8,128)(2,1)} %get-tuple-element.101.refs_6_), channel_id=1, source_target_pairs={{0,4},{1,5},{2,6},{3,7},{4,0},{5,1},{6,2},{7,3},{8,12},{9,13},{10,... | collective-permute-start | bytes 2654216 | tf_op jit(solution)/shard_map/ppermute | solution.py:418
  75.6 31.0 %collective-permute-start.4 = (bf16[288,768]{1,0:T(8,128)(2,1)}, bf16[288,768]{1,0:T(8,128)(2,1)S(1)}, u32[]{:S(2)}, u32[]{:S(2)}) collective-permute-start(bf16[288,768]{1,0:T(8,128)(2,1)} %get-tuple-element.104), channel_id=1, source_target_pairs={{0,2},{1,3},{2,0},{3,1},{4,6},{5,7},{6,4},{7,5},{8,10},{9,11},{10,... | collective-permute-start | bytes 1327112 | tf_op jit(solution)/shard_map/ppermute | solution.py:418
  86.2 28.6 %collective-permute-start.5 = (bf16[288,768]{1,0:T(8,128)(2,1)}, bf16[288,768]{1,0:T(8,128)(2,1)S(1)}, u32[]{:S(2)}, u32[]{:S(2)}) collective-permute-start(bf16[288,768]{1,0:T(8,128)(2,1)} %get-tuple-element.105), channel_id=1, source_target_pairs={{0,3},{1,2},{2,1},{3,0},{4,7},{5,6},{6,5},{7,4},{8,11},{9,10},{10,... | collective-permute-start | bytes 1327112 | tf_op jit(solution)/shard_map/ppermute | solution.py:418
  121.8 46.1 %all-to-all-start.1 = ((bf16[4,576,768]{2,1,0:T(8,128)(2,1)}), bf16[4,576,768]{2,1,0:T(8,128)(2,1)S(1)}, u32[]{:S(2)}, u32[]{:S(2)}) async-start(bf16[4,576,768]{2,1,0:T(8,128)(2,1)} %shard_map.201.refs_0_), calls=%async_computation.1 | async-start | bytes 7077888 | tf_op jit(solution)/shard_map/all_to_all | solution.py:579
  125.7 358.2 %reduce-scatter.3.cloned.1.call-start = ((), (), s32[]{:S(2)}) async-start(), calls=%async_computation.4 | async-start | bytes 5898240 | tf_op jit(solution)/shard_map/reduce_scatter | solution.py:722
  164.4 45.9 %collective-permute-start.10 = (bf16[576,768]{1,0:T(8,128)(2,1)}, bf16[576,768]{1,0:T(8,128)(2,1)}, u32[]{:S(2)}, u32[]{:S(2)}) collective-permute-start(bf16[576,768]{1,0:T(8,128)(2,1)} %get-tuple-element.114), channel_id=1, source_target_pairs={{0,1},{1,0},{2,3},{3,2},{4,5},{5,4},{6,7},{7,6},{8,9},{9,8},{10,11... | collective-permute-start | bytes 2654216 | tf_op jit(solution)/shard_map/ppermute | solution.py:418
  166.4 44.0 %collective-permute-start.11 = (bf16[576,768]{1,0:T(8,128)(2,1)}, bf16[576,768]{1,0:T(8,128)(2,1)}, u32[]{:S(2)}, u32[]{:S(2)}) collective-permute-start(bf16[576,768]{1,0:T(8,128)(2,1)} %get-tuple-element.115), channel_id=1, source_target_pairs={{0,2},{1,3},{2,0},{3,1},{4,6},{5,7},{6,4},{7,5},{8,10},{9,11},{10,... | collective-permute-start | bytes 2654216 | tf_op jit(solution)/shard_map/ppermute | solution.py:418
  167.9 42.5 %collective-permute-start.12 = (bf16[576,768]{1,0:T(8,128)(2,1)}, bf16[576,768]{1,0:T(8,128)(2,1)}, u32[]{:S(2)}, u32[]{:S(2)}) collective-permute-start(bf16[576,768]{1,0:T(8,128)(2,1)} %get-tuple-element.116), channel_id=1, source_target_pairs={{0,3},{1,2},{2,1},{3,0},{4,7},{5,6},{6,5},{7,4},{8,11},{9,10},{10,... | collective-permute-start | bytes 2654216 | tf_op jit(solution)/shard_map/ppermute | solution.py:418
  206.8 27.6 %collective-permute-start.13 = (bf16[288,768]{1,0:T(8,128)(2,1)}, bf16[288,768]{1,0:T(8,128)(2,1)S(1)}, u32[]{:S(2)}, u32[]{:S(2)}) collective-permute-start(bf16[288,768]{1,0:T(8,128)(2,1)} %get-tuple-element.121), channel_id=1, source_target_pairs={{0,1},{1,0},{2,3},{3,2},{4,5},{5,4},{6,7},{7,6},{8,9},{9,8},{10,11... | collective-permute-start | bytes 1327112 | tf_op jit(solution)/shard_map/ppermute | solution.py:418
  208.8 25.6 %collective-permute-start.14 = (bf16[288,768]{1,0:T(8,128)(2,1)}, bf16[288,768]{1,0:T(8,128)(2,1)S(1)}, u32[]{:S(2)}, u32[]{:S(2)}) collective-permute-start(bf16[288,768]{1,0:T(8,128)(2,1)} %get-tuple-element.122), channel_id=1, source_target_pairs={{0,2},{1,3},{2,0},{3,1},{4,6},{5,7},{6,4},{7,5},{8,10},{9,11},{10,... | collective-permute-start | bytes 1327112 | tf_op jit(solution)/shard_map/ppermute | solution.py:418
  210.3 24.2 %collective-permute-start.15 = (bf16[288,768]{1,0:T(8,128)(2,1)}, bf16[288,768]{1,0:T(8,128)(2,1)S(1)}, u32[]{:S(2)}, u32[]{:S(2)}) collective-permute-start(bf16[288,768]{1,0:T(8,128)(2,1)} %get-tuple-element.123), channel_id=1, source_target_pairs={{0,3},{1,2},{2,1},{3,0},{4,7},{5,6},{6,5},{7,4},{8,11},{9,10},{10,... | collective-permute-start | bytes 1327112 | tf_op jit(solution)/shard_map/ppermute | solution.py:418
  256.0 242.3 %reduce-scatter.5.cloned.1.call-start = ((), (), s32[]{:S(2)}) async-start(), calls=%async_computation.5 | async-start | bytes 5898240 | tf_op jit(solution)/shard_map/reduce_scatter | solution.py:721
  257.2 42.3 %collective-permute-start.16 = (bf16[576,768]{1,0:T(8,128)(2,1)S(1)}, bf16[576,768]{1,0:T(8,128)(2,1)S(1)}, u32[]{:S(2)}, u32[]{:S(2)}) collective-permute-start(bf16[576,768]{1,0:T(8,128)(2,1)S(1)} %copy-done.2), channel_id=1, source_target_pairs={{0,4},{1,5},{2,6},{3,7},{4,0},{5,1},{6,2},{7,3},{8,12},{9,13},{10,... | collective-permute-start | bytes 2654216 | tf_op jit(solution)/shard_map/ppermute | solution.py:418
  260.4 27.6 %collective-permute-start.18 = (bf16[288,768]{1,0:T(8,128)(2,1)S(1)}, bf16[288,768]{1,0:T(8,128)(2,1)S(1)}, u32[]{:S(2)}, u32[]{:S(2)}) collective-permute-start(bf16[288,768]{1,0:T(8,128)(2,1)S(1)} %copy-done.74), channel_id=1, source_target_pairs={{0,2},{1,3},{2,0},{3,1},{4,6},{5,7},{6,4},{7,5},{8,10},{9,11},{10,... | collective-permute-start | bytes 1327112 | tf_op jit(solution)/shard_map/ppermute | solution.py:418
  261.8 32.4 %collective-permute-start.19 = (bf16[288,768]{1,0:T(8,128)(2,1)S(1)}, bf16[288,768]{1,0:T(8,128)(2,1)S(1)}, u32[]{:S(2)}, u32[]{:S(2)}) collective-permute-start(bf16[288,768]{1,0:T(8,128)(2,1)S(1)} %copy-done.73), channel_id=1, source_target_pairs={{0,3},{1,2},{2,1},{3,0},{4,7},{5,6},{6,5},{7,4},{8,11},{9,10},{10,... | collective-permute-start | bytes 1327112 | tf_op jit(solution)/shard_map/ppermute | solution.py:418
  343.6 20.7 %collective-permute-start.53 = (bf16[384,1280]{1,0:T(8,128)(2,1)}, bf16[384,1280]{1,0:T(8,128)(2,1)S(1)}, u32[]{:S(2)}, u32[]{:S(2)}) collective-permute-start(bf16[384,1280]{1,0:T(8,128)(2,1)} %get-tuple-element.162), channel_id=1, source_target_pairs={{0,8},{8,0},{16,24},{24,16},{1,9},{9,1},{17,25},{25,17},{2,10},{10... | collective-permute-start | bytes 2949128 | tf_op jit(solution)/shard_map/ppermute | solution.py:418
  367.9 27.0 %collective-permute-start.54 = (bf16[192,1280]{1,0:T(8,128)(2,1)}, bf16[192,1280]{1,0:T(8,128)(2,1)S(1)}, u32[]{:S(2)}, u32[]{:S(2)}) collective-permute-start(bf16[192,1280]{1,0:T(8,128)(2,1)} %get-tuple-element.164), channel_id=1, source_target_pairs={{0,16},{8,24},{16,0},{24,8},{1,17},{9,25},{17,1},{25,9},{2,18},{10... | collective-permute-start | bytes 1474568 | tf_op jit(solution)/shard_map/ppermute | solution.py:418
  368.2 86.4 %collective-permute-start.21 = (bf16[576,768]{1,0:T(8,128)(2,1)S(1)}, bf16[576,768]{1,0:T(8,128)(2,1)S(1)}, u32[]{:S(2)}, u32[]{:S(2)}) collective-permute-start(bf16[576,768]{1,0:T(8,128)(2,1)S(1)} %copy-done.3), channel_id=1, source_target_pairs={{0,4},{1,5},{2,6},{3,7},{4,0},{5,1},{6,2},{7,3},{8,12},{9,13},{10,... | collective-permute-start | bytes 2654216 | tf_op jit(solution)/shard_map/ppermute | solution.py:418
  372.3 26.0 %collective-permute-start.23 = (bf16[96,896]{1,0:T(8,128)(2,1)S(1)}, bf16[96,896]{1,0:T(8,128)(2,1)S(1)}, u32[]{:S(2)}, u32[]{:S(2)}) collective-permute-start(bf16[96,896]{1,0:T(8,128)(2,1)S(1)} %copy-done.77), channel_id=1, source_target_pairs={{0,1},{1,0},{2,3},{3,2},{4,5},{5,4},{6,7},{7,6},{8,9},{9,8},{10,11... | collective-permute-start | bytes 516104 | tf_op jit(solution)/shard_map/ppermute | solution.py:418
  393.5 25.5 %collective-permute-start.39 = (bf16[96,1152]{1,0:T(8,128)(2,1)}, bf16[96,1152]{1,0:T(8,128)(2,1)S(1)}, u32[]{:S(2)}, u32[]{:S(2)}) collective-permute-start(bf16[96,1152]{1,0:T(8,128)(2,1)} %get-tuple-element.156), channel_id=1, source_target_pairs={{0,1},{1,0},{2,3},{3,2},{4,5},{5,4},{6,7},{7,6},{8,9},{9,8},{10,11... | collective-permute-start | bytes 663560 | tf_op jit(solution)/shard_map/ppermute | solution.py:418
  397.8 34.0 %collective-permute-start.55 = (bf16[96,1280]{1,0:T(8,128)(2,1)}, bf16[96,1280]{1,0:T(8,128)(2,1)S(1)}, u32[]{:S(2)}, u32[]{:S(2)}) collective-permute-start(bf16[96,1280]{1,0:T(8,128)(2,1)} %get-tuple-element.166), channel_id=1, source_target_pairs={{0,1},{1,0},{2,3},{3,2},{4,5},{5,4},{6,7},{7,6},{8,9},{9,8},{10,11... | collective-permute-start | bytes 737288 | tf_op jit(solution)/shard_map/ppermute | solution.py:418
  430.9 26.3 %collective-permute-start.31 = (bf16[96,896]{1,0:T(8,128)(2,1)}, bf16[96,896]{1,0:T(8,128)(2,1)S(1)}, u32[]{:S(2)}, u32[]{:S(2)}) collective-permute-start(bf16[96,896]{1,0:T(8,128)(2,1)} %shard_map.217.refs_3_), channel_id=1, source_target_pairs={{0,16},{8,24},{16,0},{24,8},{1,17},{9,25},{17,1},{25,9},{2,18},{10... | collective-permute-start | bytes 516104 | tf_op jit(solution)/shard_map/ppermute | solution.py:418
  436.1 22.5 %collective-permute-start.30 = (bf16[96,896]{1,0:T(8,128)(2,1)}, bf16[96,896]{1,0:T(8,128)(2,1)S(1)}, u32[]{:S(2)}, u32[]{:S(2)}) collective-permute-start(bf16[96,896]{1,0:T(8,128)(2,1)} %shard_map.217.refs_3_), channel_id=1, source_target_pairs={{0,1},{1,0},{2,3},{3,2},{4,5},{5,4},{6,7},{7,6},{8,9},{9,8},{10,11... | collective-permute-start | bytes 516104 | tf_op jit(solution)/shard_map/ppermute | solution.py:418
  (121 other events, 981.2 us)
Sparse Core Ops, SparseCore 0:
  9.6 41.5 all-gather.4
  52.8 37.4 all-gather.6
  256.1 48.0 reduce-scatter.2
  307.3 55.4 reduce-scatter.4
